TPU v7x, 32 devices: a whole 2x2x4 slice. The times are simulated.
32 devices in a mesh: feat: 16 (over z, y, x), frame: 2 (over core).
Axes of the slice: x: 2, y: 2, z: 4, core: 2. Of those that a mesh axis runs over, the one named last changes fastest.
Arguments:
- frames: float32 [6144, 440], P(('frame', 'feat')), may hold values from -6 to 6
- labels: int32 [6144], P('frame'), may hold values from 0 to 146, as said below
- proj: float32 [440, 32768], P(None, 'feat'), may hold values from -1 to 1
- phase: float32 [32768], P('feat'), may hold values from 0 to 6.2832
- class_weights: float32 [32768, 147], P('feat'), may hold values from -40 to 40
- velocity: float32 [32768, 147], P('feat'), may hold values from -3 to 3
Outputs:
- weights_out: float32 [32768, 147], P('feat')
- velocity_out: float32 [32768, 147], P('feat')
Inputs may be any that keep to these rules, and one draw needn't show every extreme that they name: labels come in runs of 4 to 12 consecutive frames that share one class (phone segments); neighbouring runs may share a class.
All inputs are finite; a program needn't handle non-finite values.
Results may differ from a plain program's by a relative error of at most 0.00011.
Values sent between devices are 32-bit elements; how exact they have to be, the bound alone decides.
No kernel may reach another device: no remote copies, remote signals or barrier semaphores. Data moves between devices by JAX's collectives and lax.ppermute only.
A program may use at most 128 MiB of HBM per device.

v0:
```python
import math

import jax
import jax.numpy as jnp
from jax import lax
from jax.sharding import PartitionSpec as P

ITERS = 2


MOMENTUM = 0.9
STEP_RATE = 0.05
EPSILON = 1e-06


def residual_of(scores, onehot):
    row_max = jnp.max(scores, axis=1, keepdims=True)
    exponent = jnp.exp(scores - row_max)
    probability = exponent / jnp.sum(exponent, axis=1, keepdims=True)
    return probability - onehot


def on_device(frames, labels, proj, phase, class_weights, velocity):
    feat_count = lax.axis_size("feat") * proj.shape[1]
    classes = class_weights.shape[1]
    feat_scale = math.sqrt(2.0 / feat_count)
    count_all = feat_count * classes
    angles = jnp.dot(
        lax.all_gather(frames, "feat", axis=0, tiled=True),
        proj,
        precision=lax.Precision.HIGHEST,
        preferred_element_type=jnp.float32,
    )
    features = feat_scale * jnp.cos(angles + phase[None, :])
    onehot = (labels[:, None] == jnp.arange(classes, dtype=jnp.int32)[None, :]).astype(jnp.float32)
    weights_now = class_weights
    velocity_now = velocity
    for iteration in range(ITERS):
        advance = weights_now + MOMENTUM * velocity_now
        partial_value = jnp.dot(
            features, advance, precision=lax.Precision.HIGHEST, preferred_element_type=jnp.float32
        )
        scores = lax.psum(partial_value, "feat")
        residual = residual_of(scores, onehot)
        grad_local = lax.dot_general(
            features,
            residual,
            (((0,), (0,)), ((), ())),
            precision=lax.Precision.HIGHEST,
            preferred_element_type=jnp.float32,
        )
        gradient = lax.psum(grad_local, "frame")
        square_sum = lax.psum(jnp.sum(gradient * gradient), "feat")
        grad_rms = jnp.sqrt(square_sum / count_all + EPSILON)
        velocity_now = MOMENTUM * velocity_now - STEP_RATE * gradient / grad_rms
        weights_now = weights_now + velocity_now
    return (weights_now, velocity_now)


def solution(mesh):
    return jax.shard_map(
        on_device,
        mesh=mesh,
        in_specs=(
            P(("frame", "feat"), None),
            P("frame"),
            P(None, "feat"),
            P("feat"),
            P("feat", None),
            P("feat", None),
        ),
        out_specs=(P("feat", None), P("feat", None)),
        check_vma=False,
    )
```

profile of v0, /device:TPU:0, one launch (start us, length us, event | category | flops | bytes accessed | tf_op | source)
XLA Modules:
  0.0 969.4 jit_solution(11034439141464893934)
XLA Ops:
  7.2 0.7 all-gather.2.cloned.1.call-update
  7.9 1.8 fusion.38
  9.8 97.9 %all-gather.2.cloned.1.call-done = f32[3072,440]{1,0:T(8,128)} async-done(((f32[192,440]{1,0:T(8,128)}), f32[3072,440]{1,0:T(8,128)}) %all-gather.2.cloned.1.call-update) | async-done | bytes 5406736 | tf_op jit(solution)/shard_map/all_gather | solution.py:29
  107.7 44.6 %fusion.28 = f32[3072,2048]{1,0:T(8,128)S(1)} fusion(f32[3072,440]{1,0:T(8,128)} %all-gather.2.cloned.1.call-done, f32[440,2048]{1,0:T(8,128)} %param.8), kind=kOutput, calls=%fused_computation.38 | convolution fusion | flops 33218887680 | bytes 34177024 | tf_op jit(solution)/shard_map/dot_general | solution.py:28
  152.4 8.3 copy-done
  160.7 113.5 %fusion.3 = f32[3072,147]{0,1:T(8,128)} fusion(f32[3072,2048]{1,0:T(8,128)S(1)} %fusion.28, f32[2048]{0:T(1024)S(1)} %copy-done.6, f32[2048,147]{0,1:T(8,128)S(1)} %fusion.38), kind=kOutput, calls=%fused_computation.4 | convolution fusion | flops 11110711296 | bytes 28184576 | tf_op jit(solution)/shard_map/dot_general | solution.py:40
  274.2 0.0 all-reduce.7.cloned.1.call-start
  274.2 121.2 %all-reduce.5.cloned.1.call-done = f32[3072,147]{0,1:T(8,128)} async-done(((f32[3072,147]{0,1:T(8,128)}), f32[3072,147]{0,1:T(8,128)}) %all-reduce.5.cloned.1.call-update) | async-done | bytes 1806352 | tf_op jit(solution)/shard_map/psum | solution.py:43
  395.4 1.7 reduce_max.18
  397.2 0.3 copy-done.2
  397.5 0.3 fusion.6
  397.8 0.4 convert_subtract_fusion.11
  398.2 99.5 %fusion.2 = f32[2048,147]{0,1:T(8,128)} fusion(f32[3072,2048]{1,0:T(8,128)} %copy-done, f32[2048]{0:T(1024)S(1)} %copy-done.6, f32[3072,147]{0,1:T(8,128)S(1)} %convert_subtract_fusion.11), kind=kOutput, calls=%fused_computation.3 | convolution fusion | flops 11110711296 | bytes 28184576 | tf_op jit(solution)/shard_map/dot_general | solution.py:45
  497.8 0.0 all-reduce.9.cloned.1.call-start
  497.8 19.3 %all-reduce.7.cloned.1.call-done = f32[2048,147]{0,1:T(8,128)} async-done(((f32[2048,147]{0,1:T(8,128)}), f32[2048,147]{0,1:T(8,128)}) %all-reduce.7.cloned.1.call-update) | async-done | bytes 1204240 | tf_op jit(solution)/shard_map/psum | solution.py:52
  517.1 2.2 multiply_reduce_fusion.1
  519.3 42.6 %psum.44 = f32[]{:T(128)} all-reduce(f32[]{:T(128)} %multiply_reduce_fusion.1), channel_id=1, replica_groups=mesh['feat'=16,'frame'=2] {'feat'}, use_global_device_ids=true, to_apply=%region_5.0 | all-reduce | flops 1 | bytes 8 | tf_op jit(solution)/shard_map/psum | solution.py:53
  562.6 2.0 fusion.27
  564.6 0.2 fusion.35
  564.8 0.8 copy-done.3
  565.6 108.2 %fusion.1 = f32[3072,147]{0,1:T(8,128)} fusion(f32[3072,2048]{1,0:T(8,128)} %copy-done, f32[2048]{0:T(1024)S(1)} %copy-done.6, f32[2048,147]{0,1:T(8,128)S(1)} %fusion.35), kind=kOutput, calls=%fused_computation.2 | convolution fusion | flops 11110711296 | bytes 28184576 | tf_op jit(solution)/shard_map/dot_general | solution.py:40
  673.9 0.0 all-reduce.11.cloned.1.call-start
  673.9 118.8 %all-reduce.9.cloned.1.call-done = f32[3072,147]{0,1:T(8,128)} async-done(((f32[3072,147]{0,1:T(8,128)}), f32[3072,147]{0,1:T(8,128)}) %all-reduce.9.cloned.1.call-update) | async-done | bytes 1806352 | tf_op jit(solution)/shard_map/psum | solution.py:43
  792.7 1.8 reduce_max.19
  794.5 0.3 copy-done.1
  794.8 0.3 fusion.7
  795.1 0.4 convert_subtract_fusion.10
  795.5 99.3 %fusion = f32[2048,147]{0,1:T(8,128)} fusion(f32[3072,2048]{1,0:T(8,128)} %copy-done, f32[2048]{0:T(1024)S(1)} %copy-done.6, f32[3072,147]{0,1:T(8,128)S(1)} %convert_subtract_fusion.10), kind=kOutput, calls=%fused_computation.1 | convolution fusion | flops 11110711296 | bytes 28184576 | tf_op jit(solution)/shard_map/dot_general | solution.py:45
  894.8 19.3 %all-reduce.11.cloned.1.call-done = f32[2048,147]{0,1:T(8,128)} async-done(((f32[2048,147]{0,1:T(8,128)}), f32[2048,147]{0,1:T(8,128)}) %all-reduce.11.cloned.1.call-update) | async-done | bytes 1204240 | tf_op jit(solution)/shard_map/psum | solution.py:52
  914.1 2.2 multiply_reduce_fusion
  916.4 42.6 %psum.47 = f32[]{:T(128)} all-reduce(f32[]{:T(128)} %multiply_reduce_fusion), channel_id=1, replica_groups=mesh['feat'=16,'frame'=2] {'feat'}, use_global_device_ids=true, to_apply=%region_11.0 | all-reduce | flops 1 | bytes 8 | tf_op jit(solution)/shard_map/psum | solution.py:53
  959.6 3.1 fusion.26
  (18 shorter events, 0.2 us)
Async XLA Ops:
  7.2 100.5 %all-gather.2.cloned.1.call-start = ((), (), s32[]{:S(2)}) async-start(), calls=%async_computation | async-start | bytes 6684672 | tf_op jit(solution)/shard_map/all_gather | solution.py:29
  7.9 387.5 %all-reduce.5.cloned.1.call-start = ((), (), s32[]{:S(2)}) async-start(), calls=%async_computation.1 | async-start | bytes 3735552 | tf_op jit(solution)/shard_map/psum | solution.py:43
  9.8 150.9 %copy-start.6 = (f32[2048]{0:T(1024)S(1)}, f32[2048]{0:T(1024)}, u32[]{:S(2)}) copy-start(f32[2048]{0:T(1024)} %param.9) | copy-start | bytes 24580
  152.3 8.3 copy-start
  274.2 123.6 %copy-start.7 = (s32[3072]{0:T(1024)S(1)}, s32[3072]{0:T(1024)}, u32[]{:S(2)}) copy-start(s32[3072]{0:T(1024)} %param.7) | copy-start | bytes 36868
  274.2 242.9 %all-reduce.7.cloned.1.call-start = ((), (), s32[]{:S(2)}) async-start(), calls=%async_computation.2 | async-start | bytes 2490368 | tf_op jit(solution)/shard_map/psum | solution.py:52
  395.4 2.1 copy-start.2
  497.7 64.8 %copy-start.5 = (f32[2048,147]{0,1:T(8,128)S(1)}, f32[2048,147]{0,1:T(8,128)}, u32[]{:S(2)}) copy-start(f32[2048,147]{0,1:T(8,128)} %param.10) | copy-start | bytes 3612676
  497.8 295.0 %all-reduce.9.cloned.1.call-start = ((), (), s32[]{:S(2)}) async-start(), calls=%async_computation.3 | async-start | bytes 3735552 | tf_op jit(solution)/shard_map/psum | solution.py:43
  564.6 1.0 copy-start.3
  673.9 240.3 %all-reduce.11.cloned.1.call-start = ((), (), s32[]{:S(2)}) async-start(), calls=%async_computation.4 | async-start | bytes 2490368 | tf_op jit(solution)/shard_map/psum | solution.py:52
  792.7 2.1 copy-start.1
  894.8 64.8 %copy-start.4 = (f32[2048,147]{0,1:T(8,128)S(1)}, f32[2048,147]{0,1:T(8,128)}, u32[]{:S(2)}) copy-start(f32[2048,147]{0,1:T(8,128)} %copy-done.3) | copy-start | bytes 3612676
Sparse Core Ops, SparseCore 0:
  10.8 96.8 all-gather.1
  274.3 121.0 all-reduce.4
  497.9 19.1 all-reduce.6
  674.0 118.7 all-reduce.8
  895.0 19.1 all-reduce.10
where the time goes:
time: 980 us; the launch traced here: 969 us
  matrix products  465 us (47%)
  waiting for transfers between devices  377 us (38%)
  blocking collectives  85.2 us (9%)
  other arithmetic  16.4 us (2%)
  between operations  15.5 us (2%)
  local copies, waits for them, and re-layouts  9.8 us (1%)
    psum x2, waiting for transfers between devices, on_device(): scores = lax.psum(partial_value, 'feat')  240 us
    dot_general x2, matrix products, on_device(): jnp.dot(features, advance, precision=lax.Precision.HIGHEST, preferred_ele...  222 us
    dot_general x2, matrix products, on_device(): lax.dot_general(features, residual, (((0,), (0,)), ((), ())), precision=l...  199 us
    all_gather x1, waiting for transfers between devices, on_device(): lax.all_gather(frames, 'feat', axis=0, tiled=True)  97.9 us
    psum x2, blocking collectives, on_device(): square_sum = lax.psum(jnp.sum(gradient * gradient), 'feat')  85.2 us
    dot_general x1, matrix products, on_device(): jnp.dot(lax.all_gather(frames, 'feat', axis=0, tiled=True), proj, precisi...  44.6 us
    psum x2, waiting for transfers between devices, on_device(): gradient = lax.psum(grad_local, 'frame')  38.6 us
  transfers between devices with their start and end apart: 5, of which 5 were waited for; matrix products, arithmetic and copies ran while one was open for 0% of the time, Pallas kernels for 0%

commit v1 on v0

v1 whole, which is shorter than its diff:
```python
import functools
import math

import jax
import jax.numpy as jnp
from jax import lax
from jax.experimental import pallas as pl
from jax.experimental.pallas import tpu as pltpu
from jax.sharding import PartitionSpec as P

ITERS = 2


MOMENTUM = 0.9
STEP_RATE = 0.05
EPSILON = 1e-06

BF16 = jnp.bfloat16
F32 = jnp.float32
NN = (((1,), (0,)), ((), ()))
NT = (((1,), (1,)), ((), ()))
MAGIC = 12582912.0
TURN = 1.0 / (2.0 * math.pi)
COS = (
    0.9999992107823203,
    -19.73898035576386,
    64.92865742102978,
    -85.2716215342655,
    58.790492119989025,
    -21.071105627426505,
)
VMEM_LIMIT = 48 * 2**20


def split(value):
    high = value.astype(BF16)
    return high, (value - high.astype(F32)).astype(BF16)


def dot(left, right, dims):
    return lax.dot_general(left, right, dims, preferred_element_type=F32)


def cos_turns(turns):
    rest = turns - ((turns + MAGIC) - MAGIC)
    square = rest * rest
    total = jnp.float32(COS[-1])
    for factor in COS[-2::-1]:
        total = total * square + jnp.float32(factor)
    return total


def pad_rows(count):
    return -(-count // 8) * 8


def features_kernel(frames, proj, phase, look, high, low, scores, proj_parts, look_parts, *, width):
    classes = look.shape[0]
    rows = scores.shape[0]

    @pl.when(pl.program_id(0) == 0)
    def _():
        proj_parts[0], proj_parts[1] = split(proj[...] * F32(TURN))
        look_parts[...] = jnp.zeros(look_parts.shape, BF16)
        look_parts[0:classes], look_parts[rows : rows + classes] = split(look[...])

    x_high, x_low = split(frames[...])
    total = jnp.zeros(scores.shape, F32)
    for start in range(0, proj.shape[1], width):
        part = slice(start, start + width)
        turns = (
            dot(x_high, proj_parts[0, :, part], NN)
            + dot(x_high, proj_parts[1, :, part], NN)
            + dot(x_low, proj_parts[0, :, part], NN)
        )
        f_high, f_low = split(cos_turns(turns + phase[:, part] * F32(TURN)))
        high[:, part] = f_high
        low[:, part] = f_low
        both = dot(look_parts[:, part], f_high, NT)
        total += both[:rows] + both[rows:] + dot(look_parts[:rows, part], f_low, NT)
    scores[...] = total


def features_call(frames, proj, phase, look, tile, width):
    count, depth = frames.shape
    feats = proj.shape[1]
    classes = look.shape[0]
    rows = pad_rows(classes)
    return pl.pallas_call(
        functools.partial(features_kernel, width=width),
        grid=(count // tile,),
        in_specs=[
            pl.BlockSpec((tile, depth), lambda i: (i, 0)),
            pl.BlockSpec((depth, feats), lambda i: (0, 0)),
            pl.BlockSpec((1, feats), lambda i: (0, 0)),
            pl.BlockSpec((classes, feats), lambda i: (0, 0)),
        ],
        out_specs=[
            pl.BlockSpec((tile, feats), lambda i: (i, 0)),
            pl.BlockSpec((tile, feats), lambda i: (i, 0)),
            pl.BlockSpec((rows, tile), lambda i: (0, i)),
        ],
        out_shape=[
            jax.ShapeDtypeStruct((count, feats), BF16),
            jax.ShapeDtypeStruct((count, feats), BF16),
            jax.ShapeDtypeStruct((rows, count), F32),
        ],
        scratch_shapes=[pltpu.VMEM((2, depth, feats), BF16), pltpu.VMEM((2 * rows, feats), BF16)],
        compiler_params=pltpu.CompilerParams(vmem_limit_bytes=VMEM_LIMIT),
        name="features",
    )(frames, proj, phase, look)


def scores_kernel(look, high, low, scores, look_parts):
    classes = look.shape[0]
    rows = scores.shape[0]

    @pl.when(pl.program_id(0) == 0)
    def _():
        look_parts[...] = jnp.zeros(look_parts.shape, BF16)
        look_parts[0:classes], look_parts[rows : rows + classes] = split(look[...])

    both = dot(look_parts[...], high[...], NT)
    scores[...] = both[:rows] + both[rows:] + dot(look_parts[:rows], low[...], NT)


def scores_call(look, high, low, tile):
    count, feats = high.shape
    classes = look.shape[0]
    rows = pad_rows(classes)
    return pl.pallas_call(
        scores_kernel,
        grid=(count // tile,),
        in_specs=[
            pl.BlockSpec((classes, feats), lambda i: (0, 0)),
            pl.BlockSpec((tile, feats), lambda i: (i, 0)),
            pl.BlockSpec((tile, feats), lambda i: (i, 0)),
        ],
        out_specs=pl.BlockSpec((rows, tile), lambda i: (0, i)),
        out_shape=jax.ShapeDtypeStruct((rows, count), F32),
        scratch_shapes=[pltpu.VMEM((2 * rows, feats), BF16)],
        compiler_params=pltpu.CompilerParams(vmem_limit_bytes=VMEM_LIMIT),
        name="scores",
    )(look, high, low)


def gradient_kernel(residual, high, low, gradient, *, width):
    rows = gradient.shape[0]

    @pl.when(pl.program_id(0) == 0)
    def _():
        gradient[...] = jnp.zeros(gradient.shape, F32)

    r_high, r_low = split(residual[...])
    r_both = jnp.concatenate([r_high, r_low], axis=0)
    for start in range(0, gradient.shape[1], width):
        part = slice(start, start + width)
        both = dot(r_both, high[:, part], NN)
        gradient[:, part] += both[:rows] + both[rows:] + dot(r_high, low[:, part], NN)


def gradient_call(residual, high, low, tile, width):
    count, feats = high.shape
    rows = residual.shape[0]
    return pl.pallas_call(
        functools.partial(gradient_kernel, width=width),
        grid=(count // tile,),
        in_specs=[
            pl.BlockSpec((rows, tile), lambda i: (0, i)),
            pl.BlockSpec((tile, feats), lambda i: (i, 0)),
            pl.BlockSpec((tile, feats), lambda i: (i, 0)),
        ],
        out_specs=pl.BlockSpec((rows, feats), lambda i: (0, 0)),
        out_shape=jax.ShapeDtypeStruct((rows, feats), F32),
        compiler_params=pltpu.CompilerParams(vmem_limit_bytes=VMEM_LIMIT),
        name="gradient",
    )(residual, high, low)


def tile_of(count, most):
    return max(t for t in range(128, most + 1, 128) if count % t == 0)


def residual_of(scores, labels, classes, scale):
    row = lax.broadcasted_iota(jnp.int32, scores.shape, 0)
    scores = jnp.where(row < classes, scores * scale, -jnp.inf)
    exponent = jnp.exp(scores - jnp.max(scores, axis=0, keepdims=True))
    probability = exponent / jnp.sum(exponent, axis=0, keepdims=True)
    return probability - (row == labels[None, :]).astype(F32)


def on_device(frames, labels, proj, phase, class_weights, velocity):
    feat_count = lax.axis_size("feat") * proj.shape[1]
    classes = class_weights.shape[1]
    feat_scale = math.sqrt(2.0 / feat_count)
    count_all = feat_count * classes
    gathered = lax.all_gather(frames, "feat", axis=0, tiled=True)
    tile = tile_of(gathered.shape[0], 512)
    weights_now = class_weights.T
    velocity_now = velocity.T
    for iteration in range(ITERS):
        advance = weights_now + MOMENTUM * velocity_now
        if iteration == 0:
            high, low, partial_value = features_call(gathered, proj, phase[None, :], advance, tile, 512)
        else:
            partial_value = scores_call(advance, high, low, tile)
        scores = lax.psum(partial_value, "feat")
        residual = residual_of(scores, labels, classes, feat_scale)
        grad_local = gradient_call(residual, high, low, tile, 512)[:classes] * feat_scale
        others = lax.axis_size("frame")
        gradient = grad_local
        moved = grad_local
        for _ in range(others - 1):
            moved = lax.ppermute(moved, "frame", [(i, (i + 1) % others) for i in range(others)])
            gradient = gradient + moved
        square_sum = lax.psum(jnp.sum(gradient * gradient), "feat")
        grad_rms = jnp.sqrt(square_sum / count_all + EPSILON)
        velocity_now = MOMENTUM * velocity_now - STEP_RATE * gradient / grad_rms
        weights_now = weights_now + velocity_now
    return (weights_now.T, velocity_now.T)


def solution(mesh):
    return jax.shard_map(
        on_device,
        mesh=mesh,
        in_specs=(
            P(("frame", "feat"), None),
            P("frame"),
            P(None, "feat"),
            P("feat"),
            P("feat", None),
            P("feat", None),
        ),
        out_specs=(P("feat", None), P("feat", None)),
        check_vma=False,
    )
```

time: 980 us -> 545 us (0.56); the launches traced: 969 us -> 545 us
  matrix products: 465 us -> 0 us
  Pallas kernels: 0 us -> 84 us
  waiting for transfers between devices: 377 us -> 345 us
    dot_general x5 -> x0, matrix products: 465 us -> none  [the longest x2 222 us: on_device(): jnp.dot(features, advance, precision=lax.Precision.HIGHEST, preferred_ele...]
    pallas_call x0 -> x4, Pallas kernels: none -> 84 us  [the longest x1 45.6 us: features_call(): pl.pallas_call(functools.partial(features_kernel, width=width), grid=(cou...]
    psum x2 -> x0, waiting for transfers between devices: 38.6 us -> none  [on_device(): gradient = lax.psum(grad_local, 'frame')]
where the time goes in v1:
time: 545 us
  waiting for transfers between devices  345 us (63%)
  Pallas kernels  84 us (15%)
  blocking collectives  81.2 us (15%)
  other arithmetic  17 us (3%)
  between operations  15.3 us (3%)
    psum x2, waiting for transfers between devices, on_device(): scores = lax.psum(partial_value, 'feat')  240 us
    all_gather x1, waiting for transfers between devices, on_device(): gathered = lax.all_gather(frames, 'feat', axis=0, tiled=True)  97.9 us
    psum x2, blocking collectives, on_device(): square_sum = lax.psum(jnp.sum(gradient * gradient), 'feat')  81.2 us
    pallas_call x1, Pallas kernels, features_call(): pl.pallas_call(functools.partial(features_kernel, width=width), grid=(cou...  45.6 us
    pallas_call x2, Pallas kernels, gradient_call(): pl.pallas_call(functools.partial(gradient_kernel, width=width), grid=(cou...  24 us
    pallas_call x1, Pallas kernels, scores_call(): pl.pallas_call(scores_kernel, grid=(count // tile,), in_specs=[pl.BlockSp...  14.3 us
  transfers between devices with their start and end apart: 5, of which 5 were waited for; matrix products, arithmetic and copies ran while one was open for 0% of the time, Pallas kernels for 0%

profile of v1, /device:TPU:0, one launch (start us, length us, event | category | flops | bytes accessed | tf_op | source)
XLA Modules:
  0.0 544.9 jit_solution(1497605312290976136)
XLA Ops:
  7.2 0.7 all-gather.2.cloned.1.call-update
  8.0 1.8 bitcast_add_fusion.look
  9.8 97.9 %all-gather.2.cloned.1.call-done.frames = f32[3072,440]{1,0:T(8,128)} async-done(((f32[192,440]{1,0:T(8,128)}), f32[3072,440]{1,0:T(8,128)}) %all-gather.2.cloned.1.call-update) | async-done | bytes 5406736 | tf_op jit(solution)/shard_map/all_gather | solution.py:197
  107.6 45.6 %features.1 = (bf16[3072,2048]{1,0:T(8,128)(2,1)}, bf16[3072,2048]{1,0:T(8,128)(2,1)}, f32[152,3072]{1,0:T(8,128)}) custom-call(f32[3072,440]{1,0:T(8,128)} %all-gather.2.cloned.1.call-done.frames, f32[440,2048]{1,0:T(8,128)} %proj.1, f32[1,2048]{1,0:T(1,128)S(1)} %bitcast.16, f32[147,2048]{1,0:T(8,128)S(1)} %bitcast_add_fusion.look), custom_call_target="tpu_custom_call" | custom-call | tf_op jit(solution)/shard_map/features/pallas_call | solution.py:89
  153.4 121.3 %all-reduce.3.cloned.1.call-done = f32[152,3072]{1,0:T(8,128)} async-done(((f32[152,3072]{1,0:T(8,128)}), f32[152,3072]{1,0:T(8,128)}) %all-reduce.3.cloned.1.call-update) | async-done | bytes 1867792 | tf_op jit(solution)/shard_map/psum | solution.py:207
  274.6 1.9 fusion
  276.6 0.1 copy-done.1
  276.7 0.5 fusion.2
  277.2 0.2 copy-done.6
  277.4 0.7 convert_subtract_fusion.1.residual
  278.1 12.0 %gradient.2 = f32[152,2048]{1,0:T(8,128)S(1)} custom-call(f32[152,3072]{1,0:T(8,128)S(1)} %convert_subtract_fusion.1.residual, bf16[3072,2048]{1,0:T(8,128)(2,1)} %get-tuple-element.6.high, bf16[3072,2048]{1,0:T(8,128)(2,1)} %get-tuple-element.7.low), custom_call_target="tpu_custom_call" | custom-call | tf_op jit(solution)/shard_map/gradient/pallas_call | solution.py:165
  290.1 0.1 slice_multiply_fusion.1
  290.3 0.1 collective-permute-start
  290.4 2.9 collective-permute-done
  293.3 1.0 copy-done.5
  294.3 0.9 multiply_reduce_fusion.1
  295.2 40.7 %psum.29 = f32[]{:T(128)} all-reduce(f32[]{:T(128)} %multiply_reduce_fusion.1), channel_id=1, replica_groups=mesh['feat'=16,'frame'=2] {'feat'}, use_global_device_ids=true, to_apply=%region_4.5 | all-reduce | flops 1 | bytes 8 | tf_op jit(solution)/shard_map/psum | solution.py:216
  336.6 3.2 multiply_add_fusion
  339.8 14.3 %scores.1 = f32[152,3072]{1,0:T(8,128)} custom-call(f32[147,2048]{1,0:T(8,128)S(1)} %get-tuple-element.8.look, bf16[3072,2048]{1,0:T(8,128)(2,1)} %get-tuple-element.6.high, bf16[3072,2048]{1,0:T(8,128)(2,1)} %get-tuple-element.7.low), custom_call_target="tpu_custom_call" | custom-call | tf_op jit(solution)/shard_map/scores/pallas_call | solution.py:131
  354.1 118.9 %all-reduce.5.cloned.1.call-done = f32[152,3072]{1,0:T(8,128)} async-done(((f32[152,3072]{1,0:T(8,128)}), f32[152,3072]{1,0:T(8,128)}) %all-reduce.5.cloned.1.call-update) | async-done | bytes 1867792 | tf_op jit(solution)/shard_map/psum | solution.py:207
  473.0 1.9 fusion.1
  475.0 0.1 copy-done.2
  475.1 0.5 fusion.3
  475.6 0.7 convert_subtract_fusion.residual
  476.3 12.0 %gradient.3 = f32[152,2048]{1,0:T(8,128)S(1)} custom-call(f32[152,3072]{1,0:T(8,128)S(1)} %convert_subtract_fusion.residual, bf16[3072,2048]{1,0:T(8,128)(2,1)} %get-tuple-element.6.high, bf16[3072,2048]{1,0:T(8,128)(2,1)} %get-tuple-element.7.low), custom_call_target="tpu_custom_call" | custom-call | tf_op jit(solution)/shard_map/gradient/pallas_call | solution.py:165
  488.3 0.1 slice_multiply_fusion
  488.4 0.1 collective-permute-start.1
  488.5 2.9 collective-permute-done.1
  491.4 1.0 copy-done.4
  492.5 1.0 multiply_reduce_fusion
  493.5 40.6 %psum.31 = f32[]{:T(128)} all-reduce(f32[]{:T(128)} %multiply_reduce_fusion), channel_id=1, replica_groups=mesh['feat'=16,'frame'=2] {'feat'}, use_global_device_ids=true, to_apply=%region_9.10 | all-reduce | flops 1 | bytes 8 | tf_op jit(solution)/shard_map/psum | solution.py:216
  534.8 3.6 fusion.4
  (15 shorter events, 0.2 us)
Async XLA Ops:
  7.2 100.5 %all-gather.2.cloned.1.call-start = ((), (), s32[]{:S(2)}) async-start(), calls=%async_computation | async-start | bytes 6684672 | tf_op jit(solution)/shard_map/all_gather | solution.py:197
  7.9 99.7 %copy-start = (f32[2048]{0:T(1024)S(1)}, f32[2048]{0:T(1024)}, u32[]{:S(2)}) copy-start(f32[2048]{0:T(1024)} %param.9) | copy-start | bytes 24580
  7.9 266.7 %all-reduce.3.cloned.1.call-start = ((), (), s32[]{:S(2)}) async-start(), calls=%async_computation.1 | async-start | bytes 3735552 | tf_op jit(solution)/shard_map/psum | solution.py:207
  153.3 319.7 %all-reduce.5.cloned.1.call-start = ((), (), s32[]{:S(2)}) async-start(), calls=%async_computation.2 | async-start | bytes 3735552 | tf_op jit(solution)/shard_map/psum | solution.py:207
  274.6 2.1 copy-start.1
  276.7 0.7 copy-start.6
  290.2 46.4 %copy-start.3 = (f32[2048,147]{0,1:T(8,128)S(1)}, f32[2048,147]{0,1:T(8,128)}, u32[]{:S(2)}) copy-start(f32[2048,147]{0,1:T(8,128)} %param.10) | copy-start | bytes 3612676
  290.3 3.0 collective-permute-start
  293.3 1.0 copy-start.5
  473.0 2.1 copy-start.2
  488.4 3.0 collective-permute-start.1
  491.4 1.0 copy-start.4
Sparse Core Ops, SparseCore 0:
  10.8 96.8 all-gather.1
  153.4 121.1 all-reduce.2
  354.2 118.7 all-reduce.4

commit v2 on v0

v2 whole, which is shorter than its diff:
```python
import functools
import math

import jax
import jax.numpy as jnp
from jax import lax
from jax.experimental import pallas as pl
from jax.experimental.pallas import tpu as pltpu
from jax.sharding import PartitionSpec as P

ITERS = 2


MOMENTUM = 0.9
STEP_RATE = 0.05
EPSILON = 1e-06

BF16 = jnp.bfloat16
F32 = jnp.float32
NN = (((1,), (0,)), ((), ()))
NT = (((1,), (1,)), ((), ()))
MAGIC = 12582912.0
TURN = 1.0 / (2.0 * math.pi)
COS = (
    0.9999992107823203,
    -19.73898035576386,
    64.92865742102978,
    -85.2716215342655,
    58.790492119989025,
    -21.071105627426505,
)
VMEM_LIMIT = 48 * 2**20
LANES = 128
GROUP = 4


def split(value):
    high = value.astype(BF16)
    return high, (value - high.astype(F32)).astype(BF16)


def split_array(value):
    high = lax.reduce_precision(value, exponent_bits=8, mantissa_bits=7)
    return high.astype(BF16), (value - high).astype(BF16)


def dot(left, right, dims):
    return lax.dot_general(left, right, dims, preferred_element_type=F32)


def cos_turns(turns):
    rest = turns - ((turns + MAGIC) - MAGIC)
    square = rest * rest
    total = jnp.float32(COS[-1])
    for factor in COS[-2::-1]:
        total = total * square + jnp.float32(factor)
    return total


def pad_rows(count):
    return -(-count // 8) * 8


def fold_plan(rows, columns):
    rest = columns % LANES
    if rest == 0 or LANES % rest or columns > 2 * LANES:
        return [((0, rows), (0, columns), 0, 0)], (rows, columns)
    whole = columns - rest
    pieces = LANES // rest
    height = pad_rows(-(-rows // pieces))
    moves = [((0, rows), (0, whole), 0, 0)] if whole else []
    base = rows if whole else 0
    for piece in range(pieces):
        top, end = piece * height, min((piece + 1) * height, rows)
        if top < end:
            moves.append(((top, end), (whole, columns), base, piece * rest))
    return moves, (base + height, LANES)


def pack_into(ref, value):
    moves, shape = fold_plan(*value.shape)
    if len(moves) > 1:
        ref[shape[0] - 8 : shape[0], :] = jnp.zeros((8, shape[1]), F32)
    for (top, end), (left, right), row, lane in moves:
        ref[row : row + end - top, lane : lane + right - left] = value[top:end, left:right]


def unpack_into(ref, start, packed, columns):
    moves, _ = fold_plan(ref.shape[0], columns)
    for (top, end), (left, right), row, lane in moves:
        ref[top:end, start + left : start + right] = packed[row : row + end - top, lane : lane + right - left]


def tree_edges(count):
    bits = count.bit_length() - 1
    assert count == 1 << bits
    loads = [0] * bits
    edges = []
    for level in range(1, bits + 1):
        nodes = [n for n in range(count) if n.bit_count() == level]
        for node in sorted(nodes, key=lambda n: -n):
            choices = [b for b in range(bits) if node >> b & 1]
            if len(choices) > 1 and choices[-1] == bits - 1:
                choices = choices[:-1]
            bit = min(choices, key=lambda b: loads[b])
            loads[bit] += 1
            edges.append((bit, node ^ (1 << bit), node))
    return edges


def swap(value, axis, bit):
    count = lax.axis_size(axis)
    return lax.ppermute(value, axis, [(i, i ^ (1 << bit)) for i in range(count)])


def spread(block, axis):
    known = {0: block}
    for bit, parent, child in tree_edges(lax.axis_size(axis)):
        known[child] = swap(known[parent], axis, bit)
    return known


def gather_sum(blocks, axis):
    total = dict(blocks)
    for bit, parent, child in reversed(tree_edges(lax.axis_size(axis))):
        total[parent] = total[parent] + swap(total[child], axis, bit)
    return total[0]


def sum_over(value, axis):
    for bit in range(lax.axis_size(axis).bit_length() - 1):
        value = value + swap(value, axis, bit)
    return value


def groups_of(axis):
    order = [0] + [child for _, _, child in tree_edges(lax.axis_size(axis))]
    return [order[i : i + GROUP] for i in range(0, len(order), GROUP)]


def features_kernel(*refs, blocks):
    frames, refs = refs[:blocks], refs[blocks:]
    p_high, p_low, phase, look, look_high, high, low = refs[:7]
    scores, (x_parts, total) = refs[7 : 7 + blocks], refs[7 + blocks :]
    columns = frames[0].shape[0]
    rows = look_high.shape[0]
    step = pl.program_id(0)

    @pl.when(step == 0)
    def _():
        for j in range(blocks):
            part = slice(j * columns, (j + 1) * columns)
            x_parts[0, part], x_parts[1, part] = split(frames[j][...])
        total[...] = jnp.zeros(total.shape, F32)

    turns = (
        dot(x_parts[0], p_high[...], NN) + dot(x_parts[0], p_low[...], NN) + dot(x_parts[1], p_high[...], NN)
    )
    f_high, f_low = split(cos_turns(turns + phase[...]))
    high[...] = f_high
    low[...] = f_low
    both = dot(look[...], f_high, NT)
    total[...] += both[:rows] + both[rows:] + dot(look_high[...], f_low, NT)

    @pl.when(step == pl.num_programs(0) - 1)
    def _():
        for j in range(blocks):
            pack_into(scores[j], total[:, j * columns : (j + 1) * columns])


def features_call(frames, proj, phase, look, width):
    blocks = len(frames)
    columns, depth = frames[0].shape
    count = blocks * columns
    feats = proj[0].shape[1]
    rows = look[1].shape[0]
    packed = fold_plan(rows, columns)[1]
    return pl.pallas_call(
        functools.partial(features_kernel, blocks=blocks),
        grid=(feats // width,),
        in_specs=[pl.BlockSpec((columns, depth), lambda i: (0, 0))] * blocks
        + [pl.BlockSpec((depth, width), lambda i: (0, i))] * 2
        + [
            pl.BlockSpec((1, width), lambda i: (0, i)),
            pl.BlockSpec((2 * rows, width), lambda i: (0, i)),
            pl.BlockSpec((rows, width), lambda i: (0, i)),
        ],
        out_specs=[pl.BlockSpec((count, width), lambda i: (0, i))] * 2
        + [pl.BlockSpec(packed, lambda i: (0, 0))] * blocks,
        out_shape=[jax.ShapeDtypeStruct((count, feats), BF16)] * 2
        + [jax.ShapeDtypeStruct(packed, F32)] * blocks,
        scratch_shapes=[pltpu.VMEM((2, count, depth), BF16), pltpu.VMEM((rows, count), F32)],
        compiler_params=pltpu.CompilerParams(vmem_limit_bytes=VMEM_LIMIT),
        cost_estimate=pl.CostEstimate(
            flops=6 * count * feats * (depth + rows), bytes_accessed=4 * count * feats, transcendentals=0
        ),
        name="features",
    )(*frames, *proj, phase, *look)


def scores_kernel(look, look_high, high, low, *refs, blocks):
    scores, total = refs[:blocks], refs[blocks]
    rows = look_high.shape[0]
    columns = total.shape[1] // blocks
    step = pl.program_id(0)

    @pl.when(step == 0)
    def _():
        total[...] = jnp.zeros(total.shape, F32)

    both = dot(look[...], high[...], NT)
    total[...] += both[:rows] + both[rows:] + dot(look_high[...], low[...], NT)

    @pl.when(step == pl.num_programs(0) - 1)
    def _():
        for j in range(blocks):
            pack_into(scores[j], total[:, j * columns : (j + 1) * columns])


def scores_call(look, high, low, blocks, width):
    count, feats = high.shape
    rows = look[1].shape[0]
    packed = fold_plan(rows, count // blocks)[1]
    return pl.pallas_call(
        functools.partial(scores_kernel, blocks=blocks),
        grid=(feats // width,),
        in_specs=[
            pl.BlockSpec((2 * rows, width), lambda i: (0, i)),
            pl.BlockSpec((rows, width), lambda i: (0, i)),
            pl.BlockSpec((count, width), lambda i: (0, i)),
            pl.BlockSpec((count, width), lambda i: (0, i)),
        ],
        out_specs=[pl.BlockSpec(packed, lambda i: (0, 0))] * blocks,
        out_shape=[jax.ShapeDtypeStruct(packed, F32)] * blocks,
        scratch_shapes=[pltpu.VMEM((rows, count), F32)],
        compiler_params=pltpu.CompilerParams(vmem_limit_bytes=VMEM_LIMIT),
        cost_estimate=pl.CostEstimate(
            flops=6 * count * feats * rows, bytes_accessed=4 * count * feats, transcendentals=0
        ),
        name="scores",
    )(*look, high, low)


def gradient_kernel(*refs, blocks, columns, first):
    residual, refs = refs[:blocks], refs[blocks:]
    if first:
        high, low, gradient, spread_out, parts = refs
    else:
        high, low, before, gradient, spread_out, parts = refs
    rows = gradient.shape[0]

    @pl.when(pl.program_id(0) == 0)
    def _():
        for j in range(blocks):
            unpack_into(spread_out, j * columns, residual[j], columns)
        r_high, r_low = split(spread_out[...])
        parts[...] = jnp.concatenate([r_high, r_low], axis=0)

    both = dot(parts[...], high[...], NN)
    value = both[:rows] + both[rows:] + dot(parts[:rows], low[...], NN)
    gradient[...] = value if first else before[...] + value


def gradient_call(residual, high, low, before, columns, rows, width):
    blocks = len(residual)
    count, feats = high.shape
    first = before is None
    return pl.pallas_call(
        functools.partial(gradient_kernel, blocks=blocks, columns=columns, first=first),
        grid=(feats // width,),
        in_specs=[pl.BlockSpec(residual[0].shape, lambda i: (0, 0))] * blocks
        + [pl.BlockSpec((count, width), lambda i: (0, i))] * 2
        + [pl.BlockSpec((rows, width), lambda i: (0, i))] * (not first),
        out_specs=pl.BlockSpec((rows, width), lambda i: (0, i)),
        out_shape=jax.ShapeDtypeStruct((rows, feats), F32),
        input_output_aliases={} if first else {blocks + 2: 0},
        scratch_shapes=[pltpu.VMEM((rows, count), F32), pltpu.VMEM((2 * rows, count), BF16)],
        compiler_params=pltpu.CompilerParams(vmem_limit_bytes=VMEM_LIMIT),
        cost_estimate=pl.CostEstimate(
            flops=6 * count * feats * rows, bytes_accessed=4 * count * feats, transcendentals=0
        ),
        name="gradient",
    )(*residual, high, low, *([] if first else [before]))


def residual_kernel(scores, labels, residual, plain, *, classes, scale):
    columns = plain.shape[1]
    unpack_into(plain, 0, scores, columns)
    row = lax.broadcasted_iota(jnp.int32, plain.shape, 0)
    value = jnp.where(row < classes, plain[...] * F32(scale), -jnp.inf)
    exponent = jnp.exp(value - jnp.max(value, axis=0, keepdims=True))
    probability = exponent / jnp.sum(exponent, axis=0, keepdims=True)
    pack_into(residual, probability - (row == labels[...]).astype(F32))


def residual_call(scores, labels, classes, scale):
    rows, columns = pad_rows(classes), labels.shape[0]
    return pl.pallas_call(
        functools.partial(residual_kernel, classes=classes, scale=scale),
        out_shape=jax.ShapeDtypeStruct(scores.shape, F32),
        scratch_shapes=[pltpu.VMEM((rows, columns), F32)],
        name="residual",
    )(scores, labels[None, :])


def look_parts(advance):
    rows = pad_rows(advance.shape[0])
    high, low = split_array(jnp.pad(advance, ((0, rows - advance.shape[0]), (0, 0))))
    return jnp.concatenate([high, low], axis=0), high


def on_device(frames, labels, proj, phase, class_weights, velocity):
    feat_count = lax.axis_size("feat") * proj.shape[1]
    classes = class_weights.shape[1]
    feat_scale = math.sqrt(2.0 / feat_count)
    count_all = feat_count * classes
    columns = frames.shape[0]
    rows = pad_rows(classes)
    groups = groups_of("feat")
    labels_own = lax.dynamic_slice(labels, (lax.axis_index("feat") * columns,), (columns,))
    known = spread(frames, "feat")
    proj_parts = split_array(proj * F32(TURN))
    phase_turns = (phase * F32(TURN))[None, :]
    weights_now = class_weights.T
    velocity_now = velocity.T
    parts = [None] * len(groups)
    for iteration in range(ITERS):
        look = look_parts(weights_now + MOMENTUM * velocity_now)
        partial_value = {}
        for g in range(len(groups)) if iteration == 0 else reversed(range(len(groups))):
            group = groups[g]
            if iteration == 0:
                high, low, *sums = features_call([known[j] for j in group], proj_parts, phase_turns, look, 512)
                parts[g] = high, low
            else:
                sums = scores_call(look, *parts[g], len(group), 512)
            partial_value.update(zip(group, sums))
        scores = gather_sum(partial_value, "feat")
        residual = spread(residual_call(scores, labels_own, classes, feat_scale), "feat")
        gradient = None
        for g, group in enumerate(groups):
            gradient = gradient_call([residual[j] for j in group], *parts[g], gradient, columns, rows, 512)
        grad_local = gradient[:classes] * feat_scale
        gradient = sum_over(grad_local, "frame")
        square_sum = sum_over(jnp.sum(gradient * gradient, keepdims=True), "feat")
        grad_rms = jnp.sqrt(square_sum / count_all + EPSILON)
        velocity_now = MOMENTUM * velocity_now - STEP_RATE * gradient / grad_rms
        weights_now = weights_now + velocity_now
    return (weights_now.T, velocity_now.T)


def solution(mesh):
    return jax.shard_map(
        on_device,
        mesh=mesh,
        in_specs=(
            P(("frame", "feat"), None),
            P("frame"),
            P(None, "feat"),
            P("feat"),
            P("feat", None),
            P("feat", None),
        ),
        out_specs=(P("feat", None), P("feat", None)),
        check_vma=False,
    )
```

time: 980 us -> 309 us (0.32)
  matrix products: 465 us -> 0 us
  waiting for transfers between devices: 377 us -> 62.9 us
  Pallas kernels: 0 us -> 112 us
  starting transfers between devices: 0.2 us -> 107 us
  blocking collectives: 85.2 us -> 0 us
    dot_general x5 -> x0, matrix products: 465 us -> none  [the longest x2 222 us: on_device(): jnp.dot(features, advance, precision=lax.Precision.HIGHEST, preferred_ele...]
    psum x4 -> x0, waiting for transfers between devices: 279 us -> none  [the longest x2 240 us: on_device(): scores = lax.psum(partial_value, 'feat')]
    pallas_call x0 -> x18, Pallas kernels: none -> 112 us  [the longest x4 52.7 us: features_call(): pl.pallas_call(functools.partial(features_kernel, blocks=blocks), grid=(f...]
    ppermute x0 -> x85, starting transfers between devices: none -> 107 us  [swap(): return lax.ppermute(value, axis, [(i, i ^ 1 << bit) for i in range(count)])]
    all_gather x1 -> x0, waiting for transfers between devices: 97.9 us -> none  [on_device(): lax.all_gather(frames, 'feat', axis=0, tiled=True)]
    psum x2 -> x0, blocking collectives: 85.2 us -> none  [on_device(): square_sum = lax.psum(jnp.sum(gradient * gradient), 'feat')]
    ppermute x0 -> x85, waiting for transfers between devices: none -> 62.9 us  [swap(): return lax.ppermute(value, axis, [(i, i ^ 1 << bit) for i in range(count)])]
  transfers between devices with their start and end apart: 5 -> 85, of which waited for: 5 -> 25; matrix products, arithmetic and copies ran while one was open for 0% -> 2% of each run, Pallas kernels for 0% -> 29%
where the time goes in v2:
time: 309 us; the launch traced here: 308 us
  Pallas kernels  112 us (36%)
  starting transfers between devices  107 us (35%)
  waiting for transfers between devices  62.9 us (20%)
  other arithmetic  14.5 us (5%)
  between operations  7.38 us (2%)
  local copies, waits for them, and re-layouts  5.06 us (2%)
    ppermute x85, starting transfers between devices, swap(): return lax.ppermute(value, axis, [(i, i ^ 1 << bit) for i in range(count)])  107 us
    ppermute x85, waiting for transfers between devices, swap(): return lax.ppermute(value, axis, [(i, i ^ 1 << bit) for i in range(count)])  62.9 us
    pallas_call x4, Pallas kernels, features_call(): pl.pallas_call(functools.partial(features_kernel, blocks=blocks), grid=(f...  52.7 us
    pallas_call x8, Pallas kernels, gradient_call(): pl.pallas_call(functools.partial(gradient_kernel, blocks=blocks, columns=...  36.2 us
    pallas_call x4, Pallas kernels, scores_call(): pl.pallas_call(functools.partial(scores_kernel, blocks=blocks), grid=(fea...  19.2 us
  transfers between devices with their start and end apart: 85, of which 25 were waited for; matrix products, arithmetic and copies ran while one was open for 2% of the time, Pallas kernels for 29%

profile of v2, /device:TPU:0, one launch (start us, length us, event | category | flops | bytes accessed | tf_op | source)
XLA Modules:
  0.0 308.1 jit_solution(780263676112485585)
XLA Ops:
  0.7 3.0 collective-permute-start.2
  9.3 4.0 %fusion = (bf16[440,2048]{1,0:T(8,128)(2,1)}, bf16[440,2048]{1,0:T(8,128)(2,1)S(1)}) fusion(f32[440,2048]{1,0:T(8,128)} %param.8), kind=kLoop, calls=%fused_computation.2 | loop fusion | flops 4505600 | bytes 7208960 | tf_op jit(solution)/shard_map/convert_element_type | solution.py:44
  13.3 11.8 %collective-permute-done.refs_1_ = f32[192,440]{1,0:T(8,128)S(1)} collective-permute-done((f32[192,440]{1,0:T(8,128)}, f32[192,440]{1,0:T(8,128)S(1)}, u32[]{:S(2)}, u32[]{:S(2)}) %collective-permute-start) | collective-permute-done | bytes 337952 | tf_op jit(solution)/shard_map/ppermute | solution.py:113
  27.6 5.3 %collective-permute-done.6.refs_3_ = f32[192,440]{1,0:T(8,128)S(1)} collective-permute-done((f32[192,440]{1,0:T(8,128)S(1)}, f32[192,440]{1,0:T(8,128)S(1)}, u32[]{:S(2)}, u32[]{:S(2)}) %collective-permute-start.6) | collective-permute-done | bytes 337952 | tf_op jit(solution)/shard_map/ppermute | solution.py:113
  38.9 3.2 %collective-permute-done.15.refs_0_ = f32[192,440]{1,0:T(8,128)S(1)} collective-permute-done((f32[192,440]{1,0:T(8,128)S(1)}, f32[192,440]{1,0:T(8,128)S(1)}, u32[]{:S(2)}, u32[]{:S(2)}) %collective-permute-start.15) | collective-permute-done | bytes 337952 | tf_op jit(solution)/shard_map/ppermute | solution.py:113
  42.7 13.1 %features.4 = (bf16[768,2048]{1,0:T(8,128)(2,1)}, bf16[768,2048]{1,0:T(8,128)(2,1)}, f32[232,128]{1,0:T(8,128)S(1)}, f32[232,128]{1,0:T(8,128)S(1)}, f32[232,128]{1,0:T(8,128)S(1)}, /*index=5*/f32[232,128]{1,0:T(8,128)S(1)}) custom-call(f32[192,440]{1,0:T(8,128)S(1)} %copy-done.10, f32[192,440]{1,0:T(8,128)S(1)} %collective-permute-done.refs_1_, ...), custom_call_target="tpu_custom_call" | custom-call | flops 5586812928 | bytes 6291456 | tf_op jit(solution)/shard_map/features/pallas_call | solution.py:178
  62.1 13.2 %features.7 = (bf16[768,2048]{1,0:T(8,128)(2,1)}, bf16[768,2048]{1,0:T(8,128)(2,1)}, f32[232,128]{1,0:T(8,128)S(1)}, f32[232,128]{1,0:T(8,128)S(1)}, f32[232,128]{1,0:T(8,128)S(1)}, /*index=5*/f32[232,128]{1,0:T(8,128)S(1)}) custom-call(f32[192,440]{1,0:T(8,128)S(1)} %collective-permute-done.15.refs_0_, f32[192,440]{1,0:T(8,128)S(1)} %collective-permute-done.16.refs_1_, ...), custom_call_target="tpu_custom_call" | custom-call | flops 5586812928 | bytes 6291456 | tf_op jit(solution)/shard_map/features/pallas_call | solution.py:178
  75.8 13.2 %features.6 = (bf16[768,2048]{1,0:T(8,128)(2,1)}, bf16[768,2048]{1,0:T(8,128)(2,1)}, f32[232,128]{1,0:T(8,128)S(1)}, f32[232,128]{1,0:T(8,128)S(1)}, f32[232,128]{1,0:T(8,128)S(1)}, /*index=5*/f32[232,128]{1,0:T(8,128)S(1)}) custom-call(f32[192,440]{1,0:T(8,128)S(1)} %collective-permute-done.8.refs_0_, f32[192,440]{1,0:T(8,128)S(1)} %collective-permute-done.9.refs_1_, ...), custom_call_target="tpu_custom_call" | custom-call | flops 5586812928 | bytes 6291456 | tf_op jit(solution)/shard_map/features/pallas_call | solution.py:178
  94.7 13.2 %features.5 = (bf16[768,2048]{1,0:T(8,128)(2,1)}, bf16[768,2048]{1,0:T(8,128)(2,1)}, f32[232,128]{1,0:T(8,128)S(1)}, f32[232,128]{1,0:T(8,128)S(1)}, f32[232,128]{1,0:T(8,128)S(1)}, /*index=5*/f32[232,128]{1,0:T(8,128)S(1)}) custom-call(f32[192,440]{1,0:T(8,128)S(1)} %collective-permute-done.3.refs_0_, f32[192,440]{1,0:T(8,128)S(1)} %collective-permute-done.4.refs_1_, ...), custom_call_target="tpu_custom_call" | custom-call | flops 5586812928 | bytes 6291456 | tf_op jit(solution)/shard_map/features/pallas_call | solution.py:178
  113.4 3.3 %collective-permute-done.14 = f32[232,128]{1,0:T(8,128)S(1)} collective-permute-done((f32[232,128]{1,0:T(8,128)S(1)}, f32[232,128]{1,0:T(8,128)S(1)}, u32[]{:S(2)}, u32[]{:S(2)}) %collective-permute-start.14) | collective-permute-done | bytes 118816 | tf_op jit(solution)/shard_map/ppermute | solution.py:113
  125.3 6.0 %collective-permute-done.29 = f32[232,128]{1,0:T(8,128)} collective-permute-done((f32[232,128]{1,0:T(8,128)S(1)}, f32[232,128]{1,0:T(8,128)}, u32[]{:S(2)}, u32[]{:S(2)}) %collective-permute-start.29) | collective-permute-done | bytes 118816 | tf_op jit(solution)/shard_map/ppermute | solution.py:113
  145.3 4.5 %gradient.8.refs_6_ = f32[152,2048]{1,0:T(8,128)S(1)} custom-call(f32[232,128]{1,0:T(8,128)S(1)} %copy-done.9, f32[232,128]{1,0:T(8,128)S(1)} %collective-permute-done.30.refs_1_, f32[232,128]{1,0:T(8,128)S(1)} %collective-permute-done.34.refs_2_, f32[232,128]{1,0:T(8,128)S(1)} %collective-permute-done.39.refs_3_, bf16[768,2048]{1,0:T(8,128)(2,1)S(1)} %copy-done.3, ...), custom_call_target="tpu_custom_call" | custom-call | flops 1434451968 | bytes 6291456 | tf_op jit(solution)/shard_map/gradient/pallas_call | solution.py:268
  154.1 4.6 %gradient.9.refs_6_ = f32[152,2048]{1,0:T(8,128)S(1)} custom-call(f32[232,128]{1,0:T(8,128)S(1)} %collective-permute-done.43.refs_0_, f32[232,128]{1,0:T(8,128)S(1)} %collective-permute-done.44.refs_1_, f32[232,128]{1,0:T(8,128)S(1)} %collective-permute-done.41.refs_2_, ...), custom_call_target="tpu_custom_call", output_to_operand_aliasing={{}: (6, {})} | custom-call | flops 1434451968 | bytes 6291456 | tf_op jit(solution)/shard_map/gradient/pallas_call | solution.py:268
  161.3 4.6 %gradient.10.refs_6_ = f32[152,2048]{1,0:T(8,128)S(1)} custom-call(f32[232,128]{1,0:T(8,128)S(1)} %collective-permute-done.35.refs_0_, f32[232,128]{1,0:T(8,128)S(1)} %collective-permute-done.38.refs_1_, f32[232,128]{1,0:T(8,128)S(1)} %collective-permute-done.40.refs_2_, ...), custom_call_target="tpu_custom_call", output_to_operand_aliasing={{}: (6, {})} | custom-call | flops 1434451968 | bytes 6291456 | tf_op jit(solution)/shard_map/gradient/pallas_call | solution.py:268
  166.0 4.4 %gradient.11 = f32[152,2048]{1,0:T(8,128)S(1)} custom-call(f32[232,128]{1,0:T(8,128)S(1)} %collective-permute-done.32.refs_0_, f32[232,128]{1,0:T(8,128)S(1)} %collective-permute-done.33.refs_1_, f32[232,128]{1,0:T(8,128)S(1)} %collective-permute-done.36.refs_2_, f32[232,128]{1,0:T(8,128)S(1)} %collective-permute-done.37.refs_3_, ...), custom_call_target="tpu_custom_call", output_to_operand_aliasing={{}: (6, {})} | custom-call | flops 1434451968 | bytes 6291456 | tf_op jit(solution)/shard_map/gradient/pallas_call | solution.py:268
  170.7 2.9 collective-permute-done.45
  179.5 2.8 collective-permute-start.47
  183.6 3.3 %collective-permute-start.48 = (f32[1,1]{1,0:T(1,128)}, f32[1,1]{1,0:T(1,128)}, u32[]{:S(2)}, u32[]{:S(2)}) collective-permute-start(f32[1,1]{1,0:T(1,128)} %add.164), channel_id=1, source_target_pairs={{0,8},{2,10},{4,12},{6,14},{8,0},{10,2},{12,4},{14,6},{16,24},{18,... | collective-permute-start | bytes 20 | tf_op jit(solution)/shard_map/ppermute | solution.py:113
  187.8 3.9 %collective-permute-start.49 = (f32[1,1]{1,0:T(1,128)}, f32[1,1]{1,0:T(1,128)}, u32[]{:S(2)}, u32[]{:S(2)}) collective-permute-start(f32[1,1]{1,0:T(1,128)} %add.165), channel_id=1, source_target_pairs={{0,16},{2,18},{4,20},{6,22},{8,24},{10,26},{12,28},{14,30},{16,0},... | collective-permute-start | bytes 20 | tf_op jit(solution)/shard_map/ppermute | solution.py:113
  194.9 4.8 %scores.7 = (f32[232,128]{1,0:T(8,128)S(1)}, f32[232,128]{1,0:T(8,128)S(1)}, f32[232,128]{1,0:T(8,128)S(1)}, f32[232,128]{1,0:T(8,128)S(1)}) custom-call(bf16[304,2048]{1,0:T(8,128)(2,1)S(1)} %pad_maximum_fusion.1.look, bf16[152,2048]{1,0:T(8,128)(2,1)S(1)} %get-tuple-element.88.look_high, bf16[768,2048]{1,0:T(8,128)(2,1)S(1)} %copy-done, ...), custom_call_target="tpu_custom_call" | custom-call | flops 1434451968 | bytes 6291456 | tf_op jit(solution)/shard_map/scores/pallas_call | solution.py:224
  199.7 4.8 %scores.6 = (f32[232,128]{1,0:T(8,128)S(1)}, f32[232,128]{1,0:T(8,128)S(1)}, f32[232,128]{1,0:T(8,128)S(1)}, f32[232,128]{1,0:T(8,128)S(1)}) custom-call(bf16[304,2048]{1,0:T(8,128)(2,1)S(1)} %pad_maximum_fusion.1.look, bf16[152,2048]{1,0:T(8,128)(2,1)S(1)} %get-tuple-element.88.look_high, bf16[768,2048]{1,0:T(8,128)(2,1)S(1)} %copy-done.1, ...), custom_call_target="tpu_custom_call" | custom-call | flops 1434451968 | bytes 6291456 | tf_op jit(solution)/shard_map/scores/pallas_call | solution.py:224
  210.5 4.9 %scores.5 = (f32[232,128]{1,0:T(8,128)S(1)}, f32[232,128]{1,0:T(8,128)S(1)}, f32[232,128]{1,0:T(8,128)S(1)}, f32[232,128]{1,0:T(8,128)S(1)}) custom-call(bf16[304,2048]{1,0:T(8,128)(2,1)S(1)} %pad_maximum_fusion.1.look, bf16[152,2048]{1,0:T(8,128)(2,1)S(1)} %get-tuple-element.88.look_high, bf16[768,2048]{1,0:T(8,128)(2,1)S(1)} %copy-done.6, ...), custom_call_target="tpu_custom_call" | custom-call | flops 1434451968 | bytes 6291456 | tf_op jit(solution)/shard_map/scores/pallas_call | solution.py:224
  215.6 4.8 %scores.4 = (f32[232,128]{1,0:T(8,128)S(1)}, f32[232,128]{1,0:T(8,128)S(1)}, f32[232,128]{1,0:T(8,128)S(1)}, f32[232,128]{1,0:T(8,128)S(1)}) custom-call(bf16[304,2048]{1,0:T(8,128)(2,1)S(1)} %pad_maximum_fusion.1.look, bf16[152,2048]{1,0:T(8,128)(2,1)S(1)} %get-tuple-element.88.look_high, bf16[768,2048]{1,0:T(8,128)(2,1)S(1)} %copy-done.4, ...), custom_call_target="tpu_custom_call" | custom-call | flops 1434451968 | bytes 6291456 | tf_op jit(solution)/shard_map/scores/pallas_call | solution.py:224
  231.3 3.1 %collective-permute-done.60 = f32[232,128]{1,0:T(8,128)S(1)} collective-permute-done((f32[232,128]{1,0:T(8,128)S(1)}, f32[232,128]{1,0:T(8,128)S(1)}, u32[]{:S(2)}, u32[]{:S(2)}) %collective-permute-start.60) | collective-permute-done | bytes 118816 | tf_op jit(solution)/shard_map/ppermute | solution.py:113
  236.0 7.1 %collective-permute-done.64 = f32[232,128]{1,0:T(8,128)S(1)} collective-permute-done((f32[232,128]{1,0:T(8,128)S(1)}, f32[232,128]{1,0:T(8,128)S(1)}, u32[]{:S(2)}, u32[]{:S(2)}) %collective-permute-start.64) | collective-permute-done | bytes 118816 | tf_op jit(solution)/shard_map/ppermute | solution.py:113
  258.1 4.5 %gradient.12.refs_6_ = f32[152,2048]{1,0:T(8,128)S(1)} custom-call(f32[232,128]{1,0:T(8,128)S(1)} %copy-done.8, f32[232,128]{1,0:T(8,128)S(1)} %collective-permute-done.65.refs_1_, f32[232,128]{1,0:T(8,128)S(1)} %collective-permute-done.69.refs_2_, f32[232,128]{1,0:T(8,128)S(1)} %collective-permute-done.74.refs_3_, bf16[768,2048]{1,0:T(8,128)(2,1)S(1)} %copy-done.5, ...), custom_call_target="tpu_custom_call" | custom-call | flops 1434451968 | bytes 6291456 | tf_op jit(solution)/shard_map/gradient/pallas_call | solution.py:268
  267.1 4.6 %gradient.13.refs_6_ = f32[152,2048]{1,0:T(8,128)S(1)} custom-call(f32[232,128]{1,0:T(8,128)S(1)} %collective-permute-done.78.refs_0_, f32[232,128]{1,0:T(8,128)S(1)} %collective-permute-done.79.refs_1_, f32[232,128]{1,0:T(8,128)S(1)} %collective-permute-done.76.refs_2_, ...), custom_call_target="tpu_custom_call", output_to_operand_aliasing={{}: (6, {})} | custom-call | flops 1434451968 | bytes 6291456 | tf_op jit(solution)/shard_map/gradient/pallas_call | solution.py:268
  274.3 4.4 %gradient.14.refs_6_ = f32[152,2048]{1,0:T(8,128)S(1)} custom-call(f32[232,128]{1,0:T(8,128)S(1)} %collective-permute-done.70.refs_0_, f32[232,128]{1,0:T(8,128)S(1)} %collective-permute-done.73.refs_1_, f32[232,128]{1,0:T(8,128)S(1)} %collective-permute-done.75.refs_2_, ...), custom_call_target="tpu_custom_call", output_to_operand_aliasing={{}: (6, {})} | custom-call | flops 1434451968 | bytes 6291456 | tf_op jit(solution)/shard_map/gradient/pallas_call | solution.py:268
  278.7 4.4 %gradient.15 = f32[152,2048]{1,0:T(8,128)S(1)} custom-call(f32[232,128]{1,0:T(8,128)S(1)} %collective-permute-done.67.refs_0_, f32[232,128]{1,0:T(8,128)S(1)} %collective-permute-done.68.refs_1_, f32[232,128]{1,0:T(8,128)S(1)} %collective-permute-done.71.refs_2_, f32[232,128]{1,0:T(8,128)S(1)} %collective-permute-done.72.refs_3_, ...), custom_call_target="tpu_custom_call", output_to_operand_aliasing={{}: (6, {})} | custom-call | flops 1434451968 | bytes 6291456 | tf_op jit(solution)/shard_map/gradient/pallas_call | solution.py:268
  283.4 2.9 collective-permute-done.80
  296.5 3.3 %collective-permute-start.83 = (f32[1,1]{1,0:T(1,128)}, f32[1,1]{1,0:T(1,128)}, u32[]{:S(2)}, u32[]{:S(2)}) collective-permute-start(f32[1,1]{1,0:T(1,128)} %add.187), channel_id=1, source_target_pairs={{0,8},{2,10},{4,12},{6,14},{8,0},{10,2},{12,4},{14,6},{16,24},{18,... | collective-permute-start | bytes 20 | tf_op jit(solution)/shard_map/ppermute | solution.py:113
  300.8 3.7 %collective-permute-start.84 = (f32[1,1]{1,0:T(1,128)}, f32[1,1]{1,0:T(1,128)}, u32[]{:S(2)}, u32[]{:S(2)}) collective-permute-start(f32[1,1]{1,0:T(1,128)} %add.188), channel_id=1, source_target_pairs={{0,16},{2,18},{4,20},{6,22},{8,24},{10,26},{12,28},{14,30},{16,0},... | collective-permute-start | bytes 20 | tf_op jit(solution)/shard_map/ppermute | solution.py:113
  (222 shorter events, 122.8 us)
Async XLA Ops:
  0.7 35.3 %collective-permute-start.2 = (f32[192,440]{1,0:T(8,128)}, f32[192,440]{1,0:T(8,128)S(1)}, u32[]{:S(2)}, u32[]{:S(2)}) collective-permute-start(f32[192,440]{1,0:T(8,128)} %refs_0_.1), channel_id=1, source_target_pairs={{0,4},{2,6},{4,0},{6,2},{8,12},{10,14},{12,8},{14,10},{16,20},{18,... | collective-permute-start | bytes 1013768 | tf_op jit(solution)/shard_map/ppermute | solution.py:113
  3.7 23.3 %collective-permute-start.1 = (f32[192,440]{1,0:T(8,128)}, f32[192,440]{1,0:T(8,128)S(1)}, u32[]{:S(2)}, u32[]{:S(2)}) collective-permute-start(f32[192,440]{1,0:T(8,128)} %refs_0_.1), channel_id=1, source_target_pairs={{0,8},{2,10},{4,12},{6,14},{8,0},{10,2},{12,4},{14,6},{16,24},{18,... | collective-permute-start | bytes 1013768 | tf_op jit(solution)/shard_map/ppermute | solution.py:113
  5.3 19.9 %collective-permute-start = (f32[192,440]{1,0:T(8,128)}, f32[192,440]{1,0:T(8,128)S(1)}, u32[]{:S(2)}, u32[]{:S(2)}) collective-permute-start(f32[192,440]{1,0:T(8,128)} %refs_0_.1), channel_id=1, source_target_pairs={{0,16},{2,18},{4,20},{6,22},{8,24},{10,26},{12,28},{14,30},{16,0},... | collective-permute-start | bytes 1013768 | tf_op jit(solution)/shard_map/ppermute | solution.py:113
  7.9 83.7 %collective-permute-start.3 = (f32[192,440]{1,0:T(8,128)}, f32[192,440]{1,0:T(8,128)S(1)}, u32[]{:S(2)}, u32[]{:S(2)}) collective-permute-start(f32[192,440]{1,0:T(8,128)} %refs_0_.1), channel_id=1, source_target_pairs={{0,2},{2,0},{4,6},{6,4},{8,10},{10,8},{12,14},{14,12},{16,18},{18,... | collective-permute-start | bytes 1013768 | tf_op jit(solution)/shard_map/ppermute | solution.py:113
  35.3 20.5 %collective-permute-start.5 = (f32[192,440]{1,0:T(8,128)S(1)}, f32[192,440]{1,0:T(8,128)S(1)}, u32[]{:S(2)}, u32[]{:S(2)}) collective-permute-start(f32[192,440]{1,0:T(8,128)S(1)} %collective-permute-done.refs_1_), channel_id=1, source_target_pairs={{0,4},{2,6},{4,0},{6,2},{8,12},{10,14},{12,8},{14,10},{16,20},{18,... | collective-permute-start | bytes 1013768 | tf_op jit(solution)/shard_map/ppermute | solution.py:113
  35.9 21.9 %collective-permute-start.16 = (f32[192,440]{1,0:T(8,128)S(1)}, f32[192,440]{1,0:T(8,128)S(1)}, u32[]{:S(2)}, u32[]{:S(2)}) collective-permute-start(f32[192,440]{1,0:T(8,128)S(1)} %collective-permute-done.6.refs_3_), channel_id=1, source_target_pairs={{0,4},{2,6},{4,0},{6,2},{8,12},{10,14},{12,8},{14,10},{16,20},{18,... | collective-permute-start | bytes 1013768 | tf_op jit(solution)/shard_map/ppermute | solution.py:113
  37.4 19.9 %collective-permute-start.17 = (f32[192,440]{1,0:T(8,128)S(1)}, f32[192,440]{1,0:T(8,128)S(1)}, u32[]{:S(2)}, u32[]{:S(2)}) collective-permute-start(f32[192,440]{1,0:T(8,128)S(1)} %collective-permute-done.8.refs_0_), channel_id=1, source_target_pairs={{0,2},{2,0},{4,6},{6,4},{8,10},{10,8},{12,14},{14,12},{16,18},{18,... | collective-permute-start | bytes 1013768 | tf_op jit(solution)/shard_map/ppermute | solution.py:113
  42.1 18.5 %collective-permute-start.18 = (f32[192,440]{1,0:T(8,128)S(1)}, f32[192,440]{1,0:T(8,128)S(1)}, u32[]{:S(2)}, u32[]{:S(2)}) collective-permute-start(f32[192,440]{1,0:T(8,128)S(1)} %collective-permute-done.15.refs_0_), channel_id=1, source_target_pairs={{0,4},{2,6},{4,0},{6,2},{8,12},{10,14},{12,8},{14,10},{16,20},{18,... | collective-permute-start | bytes 1013768 | tf_op jit(solution)/shard_map/ppermute | solution.py:113
  55.8 19.5 %collective-permute-start.10 = (f32[192,440]{1,0:T(8,128)S(1)}, f32[192,440]{1,0:T(8,128)S(1)}, u32[]{:S(2)}, u32[]{:S(2)}) collective-permute-start(f32[192,440]{1,0:T(8,128)S(1)} %collective-permute-done.2.refs_3_), channel_id=1, source_target_pairs={{0,2},{2,0},{4,6},{6,4},{8,10},{10,8},{12,14},{14,12},{16,18},{18,... | collective-permute-start | bytes 1013768 | tf_op jit(solution)/shard_map/ppermute | solution.py:113
  57.3 18.5 %collective-permute-start.9 = (f32[192,440]{1,0:T(8,128)S(1)}, f32[192,440]{1,0:T(8,128)S(1)}, u32[]{:S(2)}, u32[]{:S(2)}) collective-permute-start(f32[192,440]{1,0:T(8,128)S(1)} %collective-permute-done.1.refs_2_), channel_id=1, source_target_pairs={{0,2},{2,0},{4,6},{6,4},{8,10},{10,8},{12,14},{14,12},{16,18},{18,... | collective-permute-start | bytes 1013768 | tf_op jit(solution)/shard_map/ppermute | solution.py:113
  57.8 35.4 %collective-permute-start.4 = (f32[192,440]{1,0:T(8,128)S(1)}, f32[192,440]{1,0:T(8,128)S(1)}, u32[]{:S(2)}, u32[]{:S(2)}) collective-permute-start(f32[192,440]{1,0:T(8,128)S(1)} %collective-permute-done.refs_1_), channel_id=1, source_target_pairs={{0,8},{2,10},{4,12},{6,14},{8,0},{10,2},{12,4},{14,6},{16,24},{18,... | collective-permute-start | bytes 1013768 | tf_op jit(solution)/shard_map/ppermute | solution.py:113
  60.7 15.2 %collective-permute-start.11 = (f32[192,440]{1,0:T(8,128)S(1)}, f32[192,440]{1,0:T(8,128)S(1)}, u32[]{:S(2)}, u32[]{:S(2)}) collective-permute-start(f32[192,440]{1,0:T(8,128)S(1)} %collective-permute-done.5.refs_2_), channel_id=1, source_target_pairs={{0,8},{2,10},{4,12},{6,14},{8,0},{10,2},{12,4},{14,6},{16,24},{18,... | collective-permute-start | bytes 1013768 | tf_op jit(solution)/shard_map/ppermute | solution.py:113
  75.3 15.7 %collective-permute-start.23 = (f32[232,128]{1,0:T(8,128)S(1)}, f32[232,128]{1,0:T(8,128)S(1)}, u32[]{:S(2)}, u32[]{:S(2)}) collective-permute-start(f32[232,128]{1,0:T(8,128)S(1)} %get-tuple-element.54), channel_id=1, source_target_pairs={{0,4},{2,6},{4,0},{6,2},{8,12},{10,14},{12,8},{14,10},{16,20},{18,... | collective-permute-start | bytes 356360 | tf_op jit(solution)/shard_map/ppermute | solution.py:113
  89.0 19.5 %collective-permute-start.12 = (f32[232,128]{1,0:T(8,128)S(1)}, f32[232,128]{1,0:T(8,128)S(1)}, u32[]{:S(2)}, u32[]{:S(2)}) collective-permute-start(f32[232,128]{1,0:T(8,128)S(1)} %get-tuple-element.45), channel_id=1, source_target_pairs={{0,2},{2,0},{4,6},{6,4},{8,10},{10,8},{12,14},{14,12},{16,18},{18,... | collective-permute-start | bytes 356360 | tf_op jit(solution)/shard_map/ppermute | solution.py:113
  89.5 18.4 %collective-permute-start.26 = (f32[232,128]{1,0:T(8,128)S(1)}, f32[232,128]{1,0:T(8,128)S(1)}, u32[]{:S(2)}, u32[]{:S(2)}) collective-permute-start(f32[232,128]{1,0:T(8,128)S(1)} %get-tuple-element.56), channel_id=1, source_target_pairs={{0,8},{2,10},{4,12},{6,14},{8,0},{10,2},{12,4},{14,6},{16,24},{18,... | collective-permute-start | bytes 356360 | tf_op jit(solution)/shard_map/ppermute | solution.py:113
  91.0 19.6 %collective-permute-start.19 = (f32[232,128]{1,0:T(8,128)S(1)}, f32[232,128]{1,0:T(8,128)S(1)}, u32[]{:S(2)}, u32[]{:S(2)}) collective-permute-start(f32[232,128]{1,0:T(8,128)S(1)} %get-tuple-element.49), channel_id=1, source_target_pairs={{0,2},{2,0},{4,6},{6,4},{8,10},{10,8},{12,14},{14,12},{16,18},{18,... | collective-permute-start | bytes 356360 | tf_op jit(solution)/shard_map/ppermute | solution.py:113
  91.6 19.7 %collective-permute-start.22 = (f32[232,128]{1,0:T(8,128)S(1)}, f32[232,128]{1,0:T(8,128)S(1)}, u32[]{:S(2)}, u32[]{:S(2)}) collective-permute-start(f32[232,128]{1,0:T(8,128)S(1)} %get-tuple-element.52), channel_id=1, source_target_pairs={{0,4},{2,6},{4,0},{6,2},{8,12},{10,14},{12,8},{14,10},{16,20},{18,... | collective-permute-start | bytes 356360 | tf_op jit(solution)/shard_map/ppermute | solution.py:113
  93.2 18.6 %collective-permute-start.24 = (f32[232,128]{1,0:T(8,128)S(1)}, f32[232,128]{1,0:T(8,128)S(1)}, u32[]{:S(2)}, u32[]{:S(2)}) collective-permute-start(f32[232,128]{1,0:T(8,128)S(1)} %add.154), channel_id=1, source_target_pairs={{0,8},{2,10},{4,12},{6,14},{8,0},{10,2},{12,4},{14,6},{16,24},{18,... | collective-permute-start | bytes 356360 | tf_op jit(solution)/shard_map/ppermute | solution.py:113
  107.9 17.4 %collective-permute-start.7 = (f32[232,128]{1,0:T(8,128)S(1)}, f32[232,128]{1,0:T(8,128)}, u32[]{:S(2)}, u32[]{:S(2)}) collective-permute-start(f32[232,128]{1,0:T(8,128)S(1)} %get-tuple-element.43), channel_id=1, source_target_pairs={{0,2},{2,0},{4,6},{6,4},{8,10},{10,8},{12,14},{14,12},{16,18},{18,... | collective-permute-start | bytes 356360 | tf_op jit(solution)/shard_map/ppermute | solution.py:113
  111.3 14.0 %collective-permute-start.13 = (f32[232,128]{1,0:T(8,128)}, f32[232,128]{1,0:T(8,128)}, u32[]{:S(2)}, u32[]{:S(2)}) collective-permute-start(f32[232,128]{1,0:T(8,128)} %add.147), channel_id=1, source_target_pairs={{0,4},{2,6},{4,0},{6,2},{8,12},{10,14},{12,8},{14,10},{16,20},{18,... | collective-permute-start | bytes 356360 | tf_op jit(solution)/shard_map/ppermute | solution.py:113
  137.5 12.3 %collective-permute-start.43 = (f32[232,128]{1,0:T(8,128)}, f32[232,128]{1,0:T(8,128)S(1)}, u32[]{:S(2)}, u32[]{:S(2)}) collective-permute-start(f32[232,128]{1,0:T(8,128)} %residual.2.refs_0_), channel_id=1, source_target_pairs={{0,2},{2,0},{4,6},{6,4},{8,10},{10,8},{12,14},{14,12},{16,18},{18,... | collective-permute-start | bytes 356360 | tf_op jit(solution)/shard_map/ppermute | solution.py:113
  143.2 15.5 %collective-permute-start.40 = (f32[232,128]{1,0:T(8,128)S(1)}, f32[232,128]{1,0:T(8,128)S(1)}, u32[]{:S(2)}, u32[]{:S(2)}) collective-permute-start(f32[232,128]{1,0:T(8,128)S(1)} %collective-permute-done.39.refs_3_), channel_id=1, source_target_pairs={{0,2},{2,0},{4,6},{6,4},{8,10},{10,8},{12,14},{14,12},{16,18},{18,... | collective-permute-start | bytes 356360 | tf_op jit(solution)/shard_map/ppermute | solution.py:113
  204.5 15.9 %collective-permute-start.54 = (f32[232,128]{1,0:T(8,128)S(1)}, f32[232,128]{1,0:T(8,128)S(1)}, u32[]{:S(2)}, u32[]{:S(2)}) collective-permute-start(f32[232,128]{1,0:T(8,128)S(1)} %get-tuple-element.73), channel_id=1, source_target_pairs={{0,2},{2,0},{4,6},{6,4},{8,10},{10,8},{12,14},{14,12},{16,18},{18,... | collective-permute-start | bytes 356360 | tf_op jit(solution)/shard_map/ppermute | solution.py:113
  206.0 18.6 %collective-permute-start.57 = (f32[232,128]{1,0:T(8,128)S(1)}, f32[232,128]{1,0:T(8,128)S(1)}, u32[]{:S(2)}, u32[]{:S(2)}) collective-permute-start(f32[232,128]{1,0:T(8,128)S(1)} %get-tuple-element.76), channel_id=1, source_target_pairs={{0,4},{2,6},{4,0},{6,2},{8,12},{10,14},{12,8},{14,10},{16,20},{18,... | collective-permute-start | bytes 356360 | tf_op jit(solution)/shard_map/ppermute | solution.py:113
  208.1 13.9 %collective-permute-start.51 = (f32[232,128]{1,0:T(8,128)S(1)}, f32[232,128]{1,0:T(8,128)S(1)}, u32[]{:S(2)}, u32[]{:S(2)}) collective-permute-start(f32[232,128]{1,0:T(8,128)S(1)} %get-tuple-element.69), channel_id=1, source_target_pairs={{0,2},{2,0},{4,6},{6,4},{8,10},{10,8},{12,14},{14,12},{16,18},{18,... | collective-permute-start | bytes 356360 | tf_op jit(solution)/shard_map/ppermute | solution.py:113
  208.6 14.0 %collective-permute-start.61 = (f32[232,128]{1,0:T(8,128)S(1)}, f32[232,128]{1,0:T(8,128)S(1)}, u32[]{:S(2)}, u32[]{:S(2)}) collective-permute-start(f32[232,128]{1,0:T(8,128)S(1)} %get-tuple-element.80), channel_id=1, source_target_pairs={{0,8},{2,10},{4,12},{6,14},{8,0},{10,2},{12,4},{14,6},{16,24},{18,... | collective-permute-start | bytes 356360 | tf_op jit(solution)/shard_map/ppermute | solution.py:113
  222.0 13.2 %collective-permute-start.50 = (f32[232,128]{1,0:T(8,128)S(1)}, f32[232,128]{1,0:T(8,128)S(1)}, u32[]{:S(2)}, u32[]{:S(2)}) collective-permute-start(f32[232,128]{1,0:T(8,128)S(1)} %get-tuple-element.67), channel_id=1, source_target_pairs={{0,2},{2,0},{4,6},{6,4},{8,10},{10,8},{12,14},{14,12},{16,18},{18,... | collective-permute-start | bytes 356360 | tf_op jit(solution)/shard_map/ppermute | solution.py:113
  249.4 13.2 %collective-permute-start.78 = (f32[232,128]{1,0:T(8,128)}, f32[232,128]{1,0:T(8,128)S(1)}, u32[]{:S(2)}, u32[]{:S(2)}) collective-permute-start(f32[232,128]{1,0:T(8,128)} %residual.3.refs_0_), channel_id=1, source_target_pairs={{0,2},{2,0},{4,6},{6,4},{8,10},{10,8},{12,14},{14,12},{16,18},{18,... | collective-permute-start | bytes 356360 | tf_op jit(solution)/shard_map/ppermute | solution.py:113
  251.9 11.8 %collective-permute-start.79 = (f32[232,128]{1,0:T(8,128)S(1)}, f32[232,128]{1,0:T(8,128)S(1)}, u32[]{:S(2)}, u32[]{:S(2)}) collective-permute-start(f32[232,128]{1,0:T(8,128)S(1)} %collective-permute-done.65.refs_1_), channel_id=1, source_target_pairs={{0,8},{2,10},{4,12},{6,14},{8,0},{10,2},{12,4},{14,6},{16,24},{18,... | collective-permute-start | bytes 356360 | tf_op jit(solution)/shard_map/ppermute | solution.py:113
  251.9 13.1 %collective-permute-start.76 = (f32[232,128]{1,0:T(8,128)S(1)}, f32[232,128]{1,0:T(8,128)S(1)}, u32[]{:S(2)}, u32[]{:S(2)}) collective-permute-start(f32[232,128]{1,0:T(8,128)S(1)} %collective-permute-done.65.refs_1_), channel_id=1, source_target_pairs={{0,4},{2,6},{4,0},{6,2},{8,12},{10,14},{12,8},{14,10},{16,20},{18,... | collective-permute-start | bytes 356360 | tf_op jit(solution)/shard_map/ppermute | solution.py:113
  253.3 13.8 %collective-permute-start.66 = (f32[232,128]{1,0:T(8,128)S(1)}, f32[232,128]{1,0:T(8,128)S(1)}, u32[]{:S(2)}, u32[]{:S(2)}) collective-permute-start(f32[232,128]{1,0:T(8,128)S(1)} %collective-permute-done.65.refs_1_), channel_id=1, source_target_pairs={{0,2},{2,0},{4,6},{6,4},{8,10},{10,8},{12,14},{14,12},{16,18},{18,... | collective-permute-start | bytes 356360 | tf_op jit(solution)/shard_map/ppermute | solution.py:113
  254.3 17.4 %collective-permute-start.75 = (f32[232,128]{1,0:T(8,128)S(1)}, f32[232,128]{1,0:T(8,128)S(1)}, u32[]{:S(2)}, u32[]{:S(2)}) collective-permute-start(f32[232,128]{1,0:T(8,128)S(1)} %collective-permute-done.74.refs_3_), channel_id=1, source_target_pairs={{0,2},{2,0},{4,6},{6,4},{8,10},{10,8},{12,14},{14,12},{16,18},{18,... | collective-permute-start | bytes 356360 | tf_op jit(solution)/shard_map/ppermute | solution.py:113
  (71 other events, 604.8 us)

commit v3 on v2

v3 whole, which is shorter than its diff:
```python
import functools
import math

import jax
import jax.numpy as jnp
from jax import lax
from jax.experimental import pallas as pl
from jax.experimental.pallas import tpu as pltpu
from jax.sharding import PartitionSpec as P

ITERS = 2


MOMENTUM = 0.9
STEP_RATE = 0.05
EPSILON = 1e-06

BF16 = jnp.bfloat16
F32 = jnp.float32
NN = (((1,), (0,)), ((), ()))
NT = (((1,), (1,)), ((), ()))
MAGIC = 12582912.0
TURN = 1.0 / (2.0 * math.pi)
COS = (
    0.9999992107823203,
    -19.73898035576386,
    64.92865742102978,
    -85.2716215342655,
    58.790492119989025,
    -21.071105627426505,
)
VMEM_FEATURES = 18 * 2**20
VMEM_PRODUCTS = 16 * 2**20
VMEM_RESIDUAL = 8 * 2**20


def split(value):
    high = value.astype(BF16)
    return high, (value - high.astype(F32)).astype(BF16)


def split_array(value):
    high = lax.reduce_precision(value, exponent_bits=8, mantissa_bits=7)
    return high.astype(BF16), (value - high).astype(BF16)


def dot(left, right, dims):
    return lax.dot_general(left, right, dims, preferred_element_type=F32)


def cos_turns(turns):
    rest = turns - ((turns + MAGIC) - MAGIC)
    square = rest * rest
    total = jnp.float32(COS[-1])
    for factor in COS[-2::-1]:
        total = total * square + jnp.float32(factor)
    return total


def pad_rows(count):
    return -(-count // 8) * 8


def tree_edges(bits):
    loads, free, arrival, edges = [0] * bits, [0] * bits, {0: 0}, []
    for level in range(1, bits + 1):
        nodes = [n for n in range(1 << bits) if n.bit_count() == level]
        for node in sorted(nodes, key=lambda n: -n):
            choices = [b for b in range(bits) if node >> b & 1]
            if len(choices) > 1 and choices[-1] == bits - 1:
                choices = choices[:-1]
            bit = min(choices, key=lambda b: loads[b])
            loads[bit] += 1
            edges.append((bit, node ^ (1 << bit), node))
    ordered = []
    while edges:
        ready = [e for e in edges if e[1] in arrival]
        cost = lambda e: max(arrival[e[1]], free[e[0]]) + 1 + (e[0] == bits - 1)
        edge = min(ready, key=lambda e: (cost(e), -sum(e[2] & c[2] == e[2] for c in edges)))
        arrival[edge[2]] = free[edge[0]] = cost(edge)
        edges.remove(edge)
        ordered.append(edge)
    return ordered, arrival


def swap(value, axis, bit):
    count = lax.axis_size(axis)
    return lax.ppermute(value, axis, [(i, i ^ (1 << bit)) for i in range(count)])


def spread(item, axis, bits):
    known = {0: item}
    for bit, parent, child in tree_edges(len(bits))[0]:
        known[child] = swap(known[parent], axis, bits[bit])
    return known


def gather_sum(items, axis, bits):
    total = dict(items)
    for bit, parent, child in reversed(tree_edges(len(bits))[0]):
        total[parent] = total[parent] + swap(total[child], axis, bits[bit])
    return total[0]


def sum_over(value, axis):
    count = lax.axis_size(axis)
    bits = count.bit_length() - 1
    for low in range(0, bits, 2):
        steps = [1 << low] if low + 1 == bits else [1 << low, 2 << low, 3 << low]
        value = sum((lax.ppermute(value, axis, [(i, i ^ s) for i in range(count)]) for s in steps), value)
    return value


def units_of(axis):
    bits = lax.axis_size(axis).bit_length() - 1
    pair = bits - 2
    others = [b for b in range(bits) if b != pair]
    arrival = tree_edges(bits)[1]
    blocks = []
    for unit in range(1 << len(others)):
        first = sum((unit >> k & 1) << b for k, b in enumerate(others))
        blocks.append((first, first ^ (1 << pair)))
    order = sorted(range(len(blocks)), key=lambda u: (max(arrival[j] for j in blocks[u]), -u))
    return pair, others, blocks, [order[:1]] + [order[i : i + 2] for i in range(1, len(order), 2)]


def features_kernel(*refs, blocks):
    frames, refs = refs[:blocks], refs[blocks:]
    p_high, p_low, phase, look, look_high, _, high, low = refs[:8]
    scores, (x_parts, total) = refs[8:-2], refs[-2:]
    columns = frames[0].shape[0]
    rows = look_high.shape[0]
    step = pl.program_id(0)

    @pl.when(step == 0)
    def _():
        for j in range(blocks):
            part = slice(j * columns, (j + 1) * columns)
            x_parts[0, part], x_parts[1, part] = split(frames[j][...])
        total[...] = jnp.zeros(total.shape, F32)

    turns = (
        dot(x_parts[0], p_high[...], NN) + dot(x_parts[0], p_low[...], NN) + dot(x_parts[1], p_high[...], NN)
    )
    f_high, f_low = split(cos_turns(turns + phase[...]))
    high[...] = f_high
    low[...] = f_low
    both = dot(look[...], f_high, NT)
    total[...] += both[:rows] + both[rows:] + dot(look_high[...], f_low, NT)

    @pl.when(step == pl.num_programs(0) - 1)
    def _():
        width = 2 * columns
        for j in range(blocks // 2):
            scores[j][...] = total[:, j * width : (j + 1) * width]


def features_call(frames, proj, phase, look, after, width):
    blocks = len(frames)
    columns, depth = frames[0].shape
    count = blocks * columns
    feats = proj[0].shape[1]
    rows = look[1].shape[0]
    unit = (rows, 2 * columns)
    return pl.pallas_call(
        functools.partial(features_kernel, blocks=blocks),
        grid=(feats // width,),
        in_specs=[pl.BlockSpec((columns, depth), lambda i: (0, 0))] * blocks
        + [pl.BlockSpec((depth, width), lambda i: (0, i))] * 2
        + [
            pl.BlockSpec((1, width), lambda i: (0, i)),
            pl.BlockSpec((2 * rows, width), lambda i: (0, i)),
            pl.BlockSpec((rows, width), lambda i: (0, i)),
            pl.BlockSpec(memory_space=pl.ANY),
        ],
        out_specs=[pl.BlockSpec((count, width), lambda i: (0, i))] * 2
        + [pl.BlockSpec(unit, lambda i: (0, 0))] * (blocks // 2),
        out_shape=[jax.ShapeDtypeStruct((count, feats), BF16)] * 2
        + [jax.ShapeDtypeStruct(unit, F32)] * (blocks // 2),
        scratch_shapes=[pltpu.VMEM((2, count, depth), BF16), pltpu.VMEM((rows, count), F32)],
        compiler_params=pltpu.CompilerParams(vmem_limit_bytes=VMEM_FEATURES),
        cost_estimate=pl.CostEstimate(
            flops=6 * count * feats * (depth + rows), bytes_accessed=4 * count * feats, transcendentals=0
        ),
        name="features",
    )(*frames, *proj, phase, *look, after)


def scores_kernel(look, look_high, high, low, _, *refs):
    scores, total = refs[:-1], refs[-1]
    rows = look_high.shape[0]
    step = pl.program_id(0)

    @pl.when(step == 0)
    def _():
        total[...] = jnp.zeros(total.shape, F32)

    both = dot(look[...], high[...], NT)
    total[...] += both[:rows] + both[rows:] + dot(look_high[...], low[...], NT)

    @pl.when(step == pl.num_programs(0) - 1)
    def _():
        width = total.shape[1] // len(scores)
        for j, out in enumerate(scores):
            out[...] = total[:, j * width : (j + 1) * width]


def scores_call(look, high, low, after, units, width):
    count, feats = high.shape
    rows = look[1].shape[0]
    unit = (rows, count // units)
    return pl.pallas_call(
        scores_kernel,
        grid=(feats // width,),
        in_specs=[
            pl.BlockSpec((2 * rows, width), lambda i: (0, i)),
            pl.BlockSpec((rows, width), lambda i: (0, i)),
            pl.BlockSpec((count, width), lambda i: (0, i)),
            pl.BlockSpec((count, width), lambda i: (0, i)),
            pl.BlockSpec(memory_space=pl.ANY),
        ],
        out_specs=[pl.BlockSpec(unit, lambda i: (0, 0))] * units,
        out_shape=[jax.ShapeDtypeStruct(unit, F32)] * units,
        scratch_shapes=[pltpu.VMEM((rows, count), F32)],
        compiler_params=pltpu.CompilerParams(vmem_limit_bytes=VMEM_PRODUCTS),
        cost_estimate=pl.CostEstimate(
            flops=6 * count * feats * rows, bytes_accessed=4 * count * feats, transcendentals=0
        ),
        name="scores",
    )(*look, high, low, after)


def gradient_kernel(*refs, units, first):
    residual, refs = refs[:units], refs[units:]
    if first:
        high, low, gradient, parts = refs
    else:
        high, low, before, gradient, parts = refs
    rows, width = residual[0].shape

    @pl.when(pl.program_id(0) == 0)
    def _():
        for j in range(units):
            r_high, r_low = split(residual[j][...])
            parts[:, j * width : (j + 1) * width] = jnp.concatenate([r_high, r_low], axis=0)

    both = dot(parts[...], high[...], NN)
    value = both[:rows] + both[rows:] + dot(parts[:rows], low[...], NN)
    gradient[...] = value if first else before[...] + value


def gradient_call(residual, high, low, before, width):
    units = len(residual)
    rows = residual[0].shape[0]
    count, feats = high.shape
    first = before is None
    return pl.pallas_call(
        functools.partial(gradient_kernel, units=units, first=first),
        grid=(feats // width,),
        in_specs=[pl.BlockSpec(residual[0].shape, lambda i: (0, 0))] * units
        + [pl.BlockSpec((count, width), lambda i: (0, i))] * 2
        + [pl.BlockSpec((rows, width), lambda i: (0, i))] * (not first),
        out_specs=pl.BlockSpec((rows, width), lambda i: (0, i)),
        out_shape=jax.ShapeDtypeStruct((rows, feats), F32),
        input_output_aliases={} if first else {units + 2: 0},
        scratch_shapes=[pltpu.VMEM((2 * rows, count), BF16)],
        compiler_params=pltpu.CompilerParams(vmem_limit_bytes=VMEM_PRODUCTS),
        cost_estimate=pl.CostEstimate(
            flops=6 * count * feats * rows, bytes_accessed=4 * count * feats, transcendentals=0
        ),
        name="gradient",
    )(*residual, high, low, *([] if first else [before]))


def residual_kernel(mine, theirs, labels, residual, *, classes, scale):
    half = mine.shape[1] // 2
    row = lax.broadcasted_iota(jnp.int32, mine.shape, 0)
    turned = jnp.concatenate([theirs[:, half:], theirs[:, :half]], axis=1)
    value = jnp.where(row < classes, (mine[...] + turned) * F32(scale), -jnp.inf)
    exponent = jnp.exp(value - jnp.max(value, axis=0, keepdims=True))
    probability = exponent / jnp.sum(exponent, axis=0, keepdims=True)
    residual[...] = probability - (row == labels[...]).astype(F32)


def residual_call(mine, theirs, labels, classes, scale):
    return pl.pallas_call(
        functools.partial(residual_kernel, classes=classes, scale=scale),
        out_shape=jax.ShapeDtypeStruct(mine.shape, F32),
        compiler_params=pltpu.CompilerParams(vmem_limit_bytes=VMEM_RESIDUAL),
        name="residual",
    )(mine, theirs, labels)


def look_parts(advance):
    rows = pad_rows(advance.shape[0])
    high, low = split_array(jnp.pad(advance, ((0, rows - advance.shape[0]), (0, 0))))
    return jnp.concatenate([high, low], axis=0), high


def on_device(frames, labels, proj, phase, class_weights, velocity):
    feat_count = lax.axis_size("feat") * proj.shape[1]
    classes = class_weights.shape[1]
    feat_scale = math.sqrt(2.0 / feat_count)
    count_all = feat_count * classes
    columns = frames.shape[0]
    pair, others, blocks, groups = units_of("feat")
    me = lax.axis_index("feat")
    labels_own = jnp.concatenate(
        [lax.dynamic_slice(labels, (owner * columns,), (columns,)) for owner in (me, me ^ (1 << pair))]
    )[None, :]
    known = spread(frames, "feat", sorted(others + [pair]))
    proj_parts = split_array(proj * F32(TURN))
    phase_turns = (phase * F32(TURN))[None, :]
    weights_now = class_weights.T
    velocity_now = velocity.T
    parts = {}
    for iteration in range(ITERS):
        look = look_parts(weights_now + MOMENTUM * velocity_now)
        partial_value = {}
        after = labels_own
        order = range(len(groups))
        if iteration > 0:
            order = sorted(order, key=lambda g: -max(u.bit_count() for u in groups[g]))
        for g in order:
            if iteration == 0:
                here = [known[j] for u in groups[g] for j in blocks[u]]
                high, low, *sums = features_call(here, proj_parts, phase_turns, look, after, 512)
                parts[g] = high, low
            else:
                sums = scores_call(look, *parts[g], after, len(groups[g]), 1024)
            partial_value.update(zip(groups[g], sums))
            after = sums[0]
        mine = gather_sum(partial_value, "feat", others)
        residual = residual_call(mine, swap(mine, "feat", pair), labels_own, classes, feat_scale)
        residual = spread(residual, "feat", others)
        gradient = None
        for g in sorted(range(len(groups)), key=lambda g: max(u.bit_count() for u in groups[g])):
            gradient = gradient_call([residual[u] for u in groups[g]], *parts[g], gradient, 1024)
        gradient = sum_over(gradient[:classes] * feat_scale, "frame")
        square_sum = sum_over(jnp.sum(gradient * gradient, keepdims=True), "feat")
        grad_rms = jnp.sqrt(square_sum / count_all + EPSILON)
        velocity_now = MOMENTUM * velocity_now - STEP_RATE * gradient / grad_rms
        weights_now = weights_now + velocity_now
    return (weights_now.T, velocity_now.T)


def solution(mesh):
    return jax.shard_map(
        on_device,
        mesh=mesh,
        in_specs=(
            P(("frame", "feat"), None),
            P("frame"),
            P(None, "feat"),
            P("feat"),
            P("feat", None),
            P("feat", None),
        ),
        out_specs=(P("feat", None), P("feat", None)),
        check_vma=False,
    )
```

time: 309 us -> 258 us (0.83)
  starting transfers between devices: 107 us -> 71.1 us
  Pallas kernels: 112 us -> 85.2 us
  waiting for transfers between devices: 62.9 us -> 77.8 us
  local copies, waits for them, and re-layouts: 5.06 us -> 0.88 us
    ppermute x85 -> x45, starting transfers between devices: 107 us -> 47.3 us  [swap(): return lax.ppermute(value, axis, [(i, i ^ 1 << bit) for i in range(count)])]
    ppermute x0 -> x14, starting transfers between devices: none -> 23.8 us  [sum_over(): lax.ppermute(value, axis, [(i, i ^ s) for i in range(count)])]
    pallas_call x12 -> x15, Pallas kernels: 55.4 us -> 34.9 us  [the longest x10 22.3 us: gradient_call(): pl.pallas_call(functools.partial(gradient_kernel, units=units, first=firs...]
    ppermute x0 -> x14, waiting for transfers between devices: none -> 10.8 us  [sum_over(): lax.ppermute(value, axis, [(i, i ^ s) for i in range(count)])]
    ppermute x85 -> x45, waiting for transfers between devices: 62.9 us -> 67 us  [swap(): return lax.ppermute(value, axis, [(i, i ^ 1 << bit) for i in range(count)])]
    unnamed x36 -> x14, local copies, waits for them, and re-layouts: 3.76 us -> 0.03 us
    add x16 -> x8, other arithmetic: 4.02 us -> 0.36 us  [gather_sum(): total[parent] = total[parent] + swap(total[child], axis, bits[bit])]
    pallas_call x4 -> x5, Pallas kernels: 52.7 us -> 49.9 us  [features_call(): pl.pallas_call(functools.partial(features_kernel, blocks=blocks), grid=(f...]
  transfers between devices with their start and end apart: 85 -> 59, of which waited for: 25 -> 26; matrix products, arithmetic and copies ran while one was open for 2% -> 3% of each run, Pallas kernels for 29% -> 28%
where the time goes in v3:
time: 258 us; the launch traced here: 257 us
  Pallas kernels  85.2 us (33%)
  waiting for transfers between devices  77.8 us (30%)
  starting transfers between devices  71.1 us (28%)
  other arithmetic  12.1 us (5%)
  between operations  10.2 us (4%)
    ppermute x45, waiting for transfers between devices, swap(): return lax.ppermute(value, axis, [(i, i ^ 1 << bit) for i in range(count)])  67 us
    pallas_call x5, Pallas kernels, features_call(): pl.pallas_call(functools.partial(features_kernel, blocks=blocks), grid=(f...  49.9 us
    ppermute x45, starting transfers between devices, swap(): return lax.ppermute(value, axis, [(i, i ^ 1 << bit) for i in range(count)])  47.3 us
    ppermute x14, starting transfers between devices, sum_over(): lax.ppermute(value, axis, [(i, i ^ s) for i in range(count)])  23.8 us
    pallas_call x10, Pallas kernels, gradient_call(): pl.pallas_call(functools.partial(gradient_kernel, units=units, first=firs...  22.3 us
    pallas_call x5, Pallas kernels, scores_call(): pl.pallas_call(scores_kernel, grid=(feats // width,), in_specs=[pl.BlockS...  12.6 us
    ppermute x14, waiting for transfers between devices, sum_over(): lax.ppermute(value, axis, [(i, i ^ s) for i in range(count)])  10.8 us
    convert_element_type x3, other arithmetic, split_array(): return (high.astype(BF16), (value - high).astype(BF16))  5.31 us
  transfers between devices with their start and end apart: 59, of which 26 were waited for; matrix products, arithmetic and copies ran while one was open for 3% of the time, Pallas kernels for 28%

profile of v3, /device:TPU:0, one launch (start us, length us, event | category | flops | bytes accessed | tf_op | source)
XLA Modules:
  0.0 257.3 jit_solution(12203248068271202822)
XLA Ops:
  0.6 3.0 %collective-permute-start.5 = (f32[192,440]{1,0:T(8,128)}, f32[192,440]{1,0:T(8,128)S(1)}, u32[]{:S(2)}, u32[]{:S(2)}) collective-permute-start(f32[192,440]{1,0:T(8,128)} %refs_0_.1), channel_id=1, source_target_pairs={{0,4},{2,6},{4,0},{6,2},{8,12},{10,14},{12,8},{14,10},{16,20},{18,... | collective-permute-start | bytes 1013768 | tf_op jit(solution)/shard_map/ppermute | solution.py:88
  6.7 2.6 %collective-permute-start.1 = (f32[192,440]{1,0:T(8,128)}, f32[192,440]{1,0:T(8,128)S(1)}, u32[]{:S(2)}, u32[]{:S(2)}) collective-permute-start(f32[192,440]{1,0:T(8,128)} %refs_0_.1), channel_id=1, source_target_pairs={{0,16},{2,18},{4,20},{6,22},{8,24},{10,26},{12,28},{14,30},{16,0},... | collective-permute-start | bytes 1013768 | tf_op jit(solution)/shard_map/ppermute | solution.py:88
  9.3 4.2 %fusion = (bf16[440,2048]{1,0:T(8,128)(2,1)S(1)}, bf16[440,2048]{1,0:T(8,128)(2,1)}) fusion(f32[440,2048]{1,0:T(8,128)} %param.8), kind=kLoop, calls=%fused_computation.2 | loop fusion | flops 4505600 | bytes 7208960 | tf_op jit(solution)/shard_map/convert_element_type | solution.py:44
  16.9 4.8 %collective-permute-done.refs_1_ = f32[192,440]{1,0:T(8,128)} collective-permute-done((f32[192,440]{1,0:T(8,128)}, f32[192,440]{1,0:T(8,128)}, u32[]{:S(2)}, u32[]{:S(2)}) %collective-permute-start) | collective-permute-done | bytes 337952 | tf_op jit(solution)/shard_map/ppermute | solution.py:88
  22.0 2.6 %collective-permute-start.8 = (f32[192,440]{1,0:T(8,128)}, f32[192,440]{1,0:T(8,128)S(1)}, u32[]{:S(2)}, u32[]{:S(2)}) collective-permute-start(f32[192,440]{1,0:T(8,128)} %collective-permute-done.refs_1_), channel_id=1, source_target_pairs={{0,2},{2,0},{4,6},{6,4},{8,10},{10,8},{12,14},{14,12},{16,18},{18,... | collective-permute-start | bytes 1013768 | tf_op jit(solution)/shard_map/ppermute | solution.py:88
  27.5 7.7 %features.5 = (bf16[384,2048]{1,0:T(8,128)(2,1)S(1)}, bf16[384,2048]{1,0:T(8,128)(2,1)S(1)}, f32[152,384]{1,0:T(8,128)S(1)}) custom-call(f32[192,440]{1,0:T(8,128)S(1)} %copy-done.1, f32[192,440]{1,0:T(8,128)} %collective-permute-done.refs_1_, bf16[440,2048]{1,0:T(8,128)(2,1)S(1)} %copy-done, bf16[440,2048]{1,0:T(8,128)(2,1)S(1)} %get-tuple-element.54.refs_3_.refs_5_, ...), custom_call_target="tpu_custom_call" | custom-call | flops 2793406464 | bytes 3145728 | tf_op jit(solution)/shard_map/features/pallas_call | solution.py:165
  36.8 6.5 %collective-permute-done.9.refs_0_ = f32[192,440]{1,0:T(8,128)S(1)} collective-permute-done((f32[192,440]{1,0:T(8,128)S(1)}, f32[192,440]{1,0:T(8,128)S(1)}, u32[]{:S(2)}, u32[]{:S(2)}) %collective-permute-start.9) | collective-permute-done | bytes 337952 | tf_op jit(solution)/shard_map/ppermute | solution.py:88
  47.3 12.4 %features.6 = (bf16[768,2048]{1,0:T(8,128)(2,1)S(1)}, bf16[768,2048]{1,0:T(8,128)(2,1)S(1)}, f32[152,384]{1,0:T(8,128)S(1)}, f32[152,384]{1,0:T(8,128)S(1)}) custom-call(f32[192,440]{1,0:T(8,128)S(1)} %collective-permute-done.5.refs_0_, f32[192,440]{1,0:T(8,128)S(1)} %collective-permute-done.6.refs_1_, f32[192,440]{1,0:T(8,128)} %collective-permute-done.7.refs_2_, ...), custom_call_target="tpu_custom_call" | custom-call | flops 5586812928 | bytes 6291456 | tf_op jit(solution)/shard_map/features/pallas_call | solution.py:165
  61.8 11.5 %features.7 = (bf16[768,2048]{1,0:T(8,128)(2,1)S(1)}, bf16[768,2048]{1,0:T(8,128)(2,1)S(1)}, f32[152,384]{1,0:T(8,128)S(1)}, f32[152,384]{1,0:T(8,128)S(1)}) custom-call(f32[192,440]{1,0:T(8,128)S(1)} %collective-permute-done.1.refs_0_, f32[192,440]{1,0:T(8,128)S(1)} %collective-permute-done.2.refs_1_, f32[192,440]{1,0:T(8,128)S(1)} %collective-permute-done.3.refs_2_, ...), custom_call_target="tpu_custom_call" | custom-call | flops 5586812928 | bytes 6291456 | tf_op jit(solution)/shard_map/features/pallas_call | solution.py:165
  73.4 11.5 %features.8 = (bf16[768,2048]{1,0:T(8,128)(2,1)S(1)}, bf16[768,2048]{1,0:T(8,128)(2,1)S(1)}, f32[152,384]{1,0:T(8,128)S(1)}, f32[152,384]{1,0:T(8,128)S(1)}) custom-call(f32[192,440]{1,0:T(8,128)S(1)} %collective-permute-done.9.refs_0_, f32[192,440]{1,0:T(8,128)S(1)} %collective-permute-done.10.refs_1_, f32[192,440]{1,0:T(8,128)S(1)} %collective-permute-done.11.refs_2_, ...), custom_call_target="tpu_custom_call" | custom-call | flops 5586812928 | bytes 6291456 | tf_op jit(solution)/shard_map/features/pallas_call | solution.py:165
  84.9 6.8 %features.9 = (bf16[384,2048]{1,0:T(8,128)(2,1)S(1)}, bf16[384,2048]{1,0:T(8,128)(2,1)S(1)}, f32[152,384]{1,0:T(8,128)S(1)}) custom-call(f32[192,440]{1,0:T(8,128)S(1)} %collective-permute-done.13.refs_0_, f32[192,440]{1,0:T(8,128)S(1)} %collective-permute-done.14.refs_1_, bf16[440,2048]{1,0:T(8,128)(2,1)S(1)} %copy-done, ...), custom_call_target="tpu_custom_call" | custom-call | flops 2793406464 | bytes 3145728 | tf_op jit(solution)/shard_map/features/pallas_call | solution.py:165
  93.9 6.3 %collective-permute-done.15 = f32[152,384]{1,0:T(8,128)S(1)} collective-permute-done((f32[152,384]{1,0:T(8,128)S(1)}, f32[152,384]{1,0:T(8,128)S(1)}, u32[]{:S(2)}, u32[]{:S(2)}) %collective-permute-start.15) | collective-permute-done | bytes 233504 | tf_op jit(solution)/shard_map/ppermute | solution.py:88
  108.8 6.6 %collective-permute-done.18 = f32[152,384]{1,0:T(8,128)S(1)} collective-permute-done((f32[152,384]{1,0:T(8,128)S(1)}, f32[152,384]{1,0:T(8,128)S(1)}, u32[]{:S(2)}, u32[]{:S(2)}) %collective-permute-start.18) | collective-permute-done | bytes 233504 | tf_op jit(solution)/shard_map/ppermute | solution.py:88
  115.6 8.0 %collective-permute-done.22.theirs = f32[152,384]{1,0:T(8,128)S(1)} collective-permute-done((f32[152,384]{1,0:T(8,128)S(1)}, f32[152,384]{1,0:T(8,128)S(1)}, u32[]{:S(2)}, u32[]{:S(2)}) %collective-permute-start.22) | collective-permute-done | bytes 233504 | tf_op jit(solution)/shard_map/ppermute | solution.py:88
  126.6 5.8 %collective-permute-done.23.refs_0_ = f32[152,384]{1,0:T(8,128)S(1)} collective-permute-done((f32[152,384]{1,0:T(8,128)S(1)}, f32[152,384]{1,0:T(8,128)S(1)}, u32[]{:S(2)}, u32[]{:S(2)}) %collective-permute-start.23) | collective-permute-done | bytes 233504 | tf_op jit(solution)/shard_map/ppermute | solution.py:88
  136.9 2.5 gradient.11.refs_4_
  140.9 2.5 gradient.12.refs_4_
  143.4 2.6 gradient.13.refs_3_
  148.1 2.9 %collective-permute-done.30 = f32[147,2048]{1,0:T(8,128)S(1)} collective-permute-done((f32[147,2048]{1,0:T(8,128)S(1)}, f32[147,2048]{1,0:T(8,128)S(1)}, u32[]{:S(2)}, u32[]{:S(2)}) %collective-permute-start.30) | collective-permute-done | bytes 1204256 | tf_op jit(solution)/shard_map/ppermute | solution.py:110
  160.2 4.5 %collective-permute-start.35 = (f32[1,1]{1,0:T(1,128)}, f32[1,1]{1,0:T(1,128)}, u32[]{:S(2)}, u32[]{:S(2)}) collective-permute-start(f32[1,1]{1,0:T(1,128)} %add.125), channel_id=1, source_target_pairs={{0,16},{2,18},{4,20},{6,22},{8,24},{10,26},{12,28},{14,30},{16,0},... | collective-permute-start | bytes 20 | tf_op jit(solution)/shard_map/ppermute | solution.py:110
  174.7 2.9 %scores.6 = (f32[152,384]{1,0:T(8,128)S(1)}, f32[152,384]{1,0:T(8,128)S(1)}) custom-call(bf16[304,2048]{1,0:T(8,128)(2,1)S(1)} %pad_maximum_fusion.1.look, bf16[152,2048]{1,0:T(8,128)(2,1)S(1)} %get-tuple-element.56.look_high, bf16[768,2048]{1,0:T(8,128)(2,1)S(1)} %get-tuple-element.38.refs_2_.high, bf16[768,2048]{1,0:T(8,128)(2,1)S(1)} %get-tuple-element.39.refs_3_.low, ...), custom_call_target="tpu_custom_call" | custom-call | flops 1434451968 | bytes 6291456 | tf_op jit(solution)/shard_map/scores/pallas_call | solution.py:212
  177.6 2.9 %scores.7 = (f32[152,384]{1,0:T(8,128)S(1)}, f32[152,384]{1,0:T(8,128)S(1)}) custom-call(bf16[304,2048]{1,0:T(8,128)(2,1)S(1)} %pad_maximum_fusion.1.look, bf16[152,2048]{1,0:T(8,128)(2,1)S(1)} %get-tuple-element.56.look_high, bf16[768,2048]{1,0:T(8,128)(2,1)S(1)} %get-tuple-element.36.refs_2_.high, bf16[768,2048]{1,0:T(8,128)(2,1)S(1)} %get-tuple-element.37.refs_3_.low, ...), custom_call_target="tpu_custom_call" | custom-call | flops 1434451968 | bytes 6291456 | tf_op jit(solution)/shard_map/scores/pallas_call | solution.py:212
  183.6 2.9 %scores.8 = (f32[152,384]{1,0:T(8,128)S(1)}, f32[152,384]{1,0:T(8,128)S(1)}) custom-call(bf16[304,2048]{1,0:T(8,128)(2,1)S(1)} %pad_maximum_fusion.1.look, bf16[152,2048]{1,0:T(8,128)(2,1)S(1)} %get-tuple-element.56.look_high, bf16[768,2048]{1,0:T(8,128)(2,1)S(1)} %get-tuple-element.40.refs_2_.high, bf16[768,2048]{1,0:T(8,128)(2,1)S(1)} %get-tuple-element.41.refs_3_.low, ...), custom_call_target="tpu_custom_call" | custom-call | flops 1434451968 | bytes 6291456 | tf_op jit(solution)/shard_map/scores/pallas_call | solution.py:212
  195.2 5.1 %collective-permute-done.40 = f32[152,384]{1,0:T(8,128)S(1)} collective-permute-done((f32[152,384]{1,0:T(8,128)S(1)}, f32[152,384]{1,0:T(8,128)S(1)}, u32[]{:S(2)}, u32[]{:S(2)}) %collective-permute-start.40) | collective-permute-done | bytes 233504 | tf_op jit(solution)/shard_map/ppermute | solution.py:88
  200.4 7.8 %collective-permute-done.44.theirs = f32[152,384]{1,0:T(8,128)S(1)} collective-permute-done((f32[152,384]{1,0:T(8,128)S(1)}, f32[152,384]{1,0:T(8,128)S(1)}, u32[]{:S(2)}, u32[]{:S(2)}) %collective-permute-start.44) | collective-permute-done | bytes 233504 | tf_op jit(solution)/shard_map/ppermute | solution.py:88
  211.1 5.9 %collective-permute-done.45.refs_0_ = f32[152,384]{1,0:T(8,128)S(1)} collective-permute-done((f32[152,384]{1,0:T(8,128)S(1)}, f32[152,384]{1,0:T(8,128)S(1)}, u32[]{:S(2)}, u32[]{:S(2)}) %collective-permute-start.45) | collective-permute-done | bytes 233504 | tf_op jit(solution)/shard_map/ppermute | solution.py:88
  221.7 2.5 gradient.16.refs_4_
  225.5 2.5 gradient.17.refs_4_
  228.0 2.6 gradient.18.refs_3_
  232.6 2.9 %collective-permute-done.52 = f32[147,2048]{1,0:T(8,128)S(1)} collective-permute-done((f32[147,2048]{1,0:T(8,128)S(1)}, f32[147,2048]{1,0:T(8,128)S(1)}, u32[]{:S(2)}, u32[]{:S(2)}) %collective-permute-start.52) | collective-permute-done | bytes 1204256 | tf_op jit(solution)/shard_map/ppermute | solution.py:110
  245.5 3.8 %collective-permute-start.57 = (f32[1,1]{1,0:T(1,128)}, f32[1,1]{1,0:T(1,128)}, u32[]{:S(2)}, u32[]{:S(2)}) collective-permute-start(f32[1,1]{1,0:T(1,128)} %add.142), channel_id=1, source_target_pairs={{0,16},{2,18},{4,20},{6,22},{8,24},{10,26},{12,28},{14,30},{16,0},... | collective-permute-start | bytes 20 | tf_op jit(solution)/shard_map/ppermute | solution.py:110
  249.3 3.2 %collective-permute-start.58 = (f32[1,1]{1,0:T(1,128)}, f32[1,1]{1,0:T(1,128)}, u32[]{:S(2)}, u32[]{:S(2)}) collective-permute-start(f32[1,1]{1,0:T(1,128)} %add.142), channel_id=1, source_target_pairs={{0,24},{2,26},{4,28},{6,30},{8,16},{10,18},{12,20},{14,22},{16,8},... | collective-permute-start | bytes 20 | tf_op jit(solution)/shard_map/ppermute | solution.py:110
  (146 shorter events, 87.0 us)
Async XLA Ops:
  0.6 26.3 %collective-permute-start.5 = (f32[192,440]{1,0:T(8,128)}, f32[192,440]{1,0:T(8,128)S(1)}, u32[]{:S(2)}, u32[]{:S(2)}) collective-permute-start(f32[192,440]{1,0:T(8,128)} %refs_0_.1), channel_id=1, source_target_pairs={{0,4},{2,6},{4,0},{6,2},{8,12},{10,14},{12,8},{14,10},{16,20},{18,... | collective-permute-start | bytes 1013768 | tf_op jit(solution)/shard_map/ppermute | solution.py:88
  3.7 18.0 %collective-permute-start = (f32[192,440]{1,0:T(8,128)}, f32[192,440]{1,0:T(8,128)}, u32[]{:S(2)}, u32[]{:S(2)}) collective-permute-start(f32[192,440]{1,0:T(8,128)} %refs_0_.1), channel_id=1, source_target_pairs={{0,8},{2,10},{4,12},{6,14},{8,0},{10,2},{12,4},{14,6},{16,24},{18,... | collective-permute-start | bytes 1013768 | tf_op jit(solution)/shard_map/ppermute | solution.py:88
  5.2 29.9 %collective-permute-start.7 = (f32[192,440]{1,0:T(8,128)}, f32[192,440]{1,0:T(8,128)}, u32[]{:S(2)}, u32[]{:S(2)}) collective-permute-start(f32[192,440]{1,0:T(8,128)} %refs_0_.1), channel_id=1, source_target_pairs={{0,2},{2,0},{4,6},{6,4},{8,10},{10,8},{12,14},{14,12},{16,18},{18,... | collective-permute-start | bytes 1013768 | tf_op jit(solution)/shard_map/ppermute | solution.py:88
  6.7 19.6 %collective-permute-start.1 = (f32[192,440]{1,0:T(8,128)}, f32[192,440]{1,0:T(8,128)S(1)}, u32[]{:S(2)}, u32[]{:S(2)}) collective-permute-start(f32[192,440]{1,0:T(8,128)} %refs_0_.1), channel_id=1, source_target_pairs={{0,16},{2,18},{4,20},{6,22},{8,24},{10,26},{12,28},{14,30},{16,0},... | collective-permute-start | bytes 1013768 | tf_op jit(solution)/shard_map/ppermute | solution.py:88
  21.6 13.8 %collective-permute-start.6 = (f32[192,440]{1,0:T(8,128)}, f32[192,440]{1,0:T(8,128)S(1)}, u32[]{:S(2)}, u32[]{:S(2)}) collective-permute-start(f32[192,440]{1,0:T(8,128)} %collective-permute-done.refs_1_), channel_id=1, source_target_pairs={{0,4},{2,6},{4,0},{6,2},{8,12},{10,14},{12,8},{14,10},{16,20},{18,... | collective-permute-start | bytes 1013768 | tf_op jit(solution)/shard_map/ppermute | solution.py:88
  22.0 21.3 %collective-permute-start.8 = (f32[192,440]{1,0:T(8,128)}, f32[192,440]{1,0:T(8,128)S(1)}, u32[]{:S(2)}, u32[]{:S(2)}) collective-permute-start(f32[192,440]{1,0:T(8,128)} %collective-permute-done.refs_1_), channel_id=1, source_target_pairs={{0,2},{2,0},{4,6},{6,4},{8,10},{10,8},{12,14},{14,12},{16,18},{18,... | collective-permute-start | bytes 1013768 | tf_op jit(solution)/shard_map/ppermute | solution.py:88
  26.3 16.9 %collective-permute-start.9 = (f32[192,440]{1,0:T(8,128)S(1)}, f32[192,440]{1,0:T(8,128)S(1)}, u32[]{:S(2)}, u32[]{:S(2)}) collective-permute-start(f32[192,440]{1,0:T(8,128)S(1)} %collective-permute-done.1.refs_0_), channel_id=1, source_target_pairs={{0,2},{2,0},{4,6},{6,4},{8,10},{10,8},{12,14},{14,12},{16,18},{18,... | collective-permute-start | bytes 1013768 | tf_op jit(solution)/shard_map/ppermute | solution.py:88
  26.9 18.4 %collective-permute-start.3 = (f32[192,440]{1,0:T(8,128)S(1)}, f32[192,440]{1,0:T(8,128)S(1)}, u32[]{:S(2)}, u32[]{:S(2)}) collective-permute-start(f32[192,440]{1,0:T(8,128)S(1)} %collective-permute-done.1.refs_0_), channel_id=1, source_target_pairs={{0,4},{2,6},{4,0},{6,2},{8,12},{10,14},{12,8},{14,10},{16,20},{18,... | collective-permute-start | bytes 1013768 | tf_op jit(solution)/shard_map/ppermute | solution.py:88
  35.2 24.6 %collective-permute-start.2 = (f32[192,440]{1,0:T(8,128)S(1)}, f32[192,440]{1,0:T(8,128)S(1)}, u32[]{:S(2)}, u32[]{:S(2)}) collective-permute-start(f32[192,440]{1,0:T(8,128)S(1)} %collective-permute-done.1.refs_0_), channel_id=1, source_target_pairs={{0,8},{2,10},{4,12},{6,14},{8,0},{10,2},{12,4},{14,6},{16,24},{18,... | collective-permute-start | bytes 1013768 | tf_op jit(solution)/shard_map/ppermute | solution.py:88
  35.4 38.0 %collective-permute-start.11 = (f32[192,440]{1,0:T(8,128)S(1)}, f32[192,440]{1,0:T(8,128)S(1)}, u32[]{:S(2)}, u32[]{:S(2)}) collective-permute-start(f32[192,440]{1,0:T(8,128)S(1)} %collective-permute-done.5.refs_0_), channel_id=1, source_target_pairs={{0,2},{2,0},{4,6},{6,4},{8,10},{10,8},{12,14},{14,12},{16,18},{18,... | collective-permute-start | bytes 1013768 | tf_op jit(solution)/shard_map/ppermute | solution.py:88
  43.3 18.0 %collective-permute-start.10 = (f32[192,440]{1,0:T(8,128)S(1)}, f32[192,440]{1,0:T(8,128)S(1)}, u32[]{:S(2)}, u32[]{:S(2)}) collective-permute-start(f32[192,440]{1,0:T(8,128)S(1)} %collective-permute-done.9.refs_0_), channel_id=1, source_target_pairs={{0,8},{2,10},{4,12},{6,14},{8,0},{10,2},{12,4},{14,6},{16,24},{18,... | collective-permute-start | bytes 1013768 | tf_op jit(solution)/shard_map/ppermute | solution.py:88
  43.3 30.1 %collective-permute-start.12 = (f32[192,440]{1,0:T(8,128)S(1)}, f32[192,440]{1,0:T(8,128)S(1)}, u32[]{:S(2)}, u32[]{:S(2)}) collective-permute-start(f32[192,440]{1,0:T(8,128)S(1)} %collective-permute-done.6.refs_1_), channel_id=1, source_target_pairs={{0,2},{2,0},{4,6},{6,4},{8,10},{10,8},{12,14},{14,12},{16,18},{18,... | collective-permute-start | bytes 1013768 | tf_op jit(solution)/shard_map/ppermute | solution.py:88
  45.3 16.5 %collective-permute-start.4 = (f32[192,440]{1,0:T(8,128)S(1)}, f32[192,440]{1,0:T(8,128)S(1)}, u32[]{:S(2)}, u32[]{:S(2)}) collective-permute-start(f32[192,440]{1,0:T(8,128)S(1)} %collective-permute-done.3.refs_2_), channel_id=1, source_target_pairs={{0,8},{2,10},{4,12},{6,14},{8,0},{10,2},{12,4},{14,6},{16,24},{18,... | collective-permute-start | bytes 1013768 | tf_op jit(solution)/shard_map/ppermute | solution.py:88
  59.7 25.2 %collective-permute-start.13 = (f32[192,440]{1,0:T(8,128)S(1)}, f32[192,440]{1,0:T(8,128)S(1)}, u32[]{:S(2)}, u32[]{:S(2)}) collective-permute-start(f32[192,440]{1,0:T(8,128)S(1)} %collective-permute-done.9.refs_0_), channel_id=1, source_target_pairs={{0,4},{2,6},{4,0},{6,2},{8,12},{10,14},{12,8},{14,10},{16,20},{18,... | collective-permute-start | bytes 1013768 | tf_op jit(solution)/shard_map/ppermute | solution.py:88
  61.3 23.6 %collective-permute-start.14 = (f32[192,440]{1,0:T(8,128)S(1)}, f32[192,440]{1,0:T(8,128)S(1)}, u32[]{:S(2)}, u32[]{:S(2)}) collective-permute-start(f32[192,440]{1,0:T(8,128)S(1)} %collective-permute-done.10.refs_1_), channel_id=1, source_target_pairs={{0,4},{2,6},{4,0},{6,2},{8,12},{10,14},{12,8},{14,10},{16,20},{18,... | collective-permute-start | bytes 1013768 | tf_op jit(solution)/shard_map/ppermute | solution.py:88
  91.7 8.5 %collective-permute-start.15 = (f32[152,384]{1,0:T(8,128)S(1)}, f32[152,384]{1,0:T(8,128)S(1)}, u32[]{:S(2)}, u32[]{:S(2)}) collective-permute-start(f32[152,384]{1,0:T(8,128)S(1)} %get-tuple-element.30), channel_id=1, source_target_pairs={{0,4},{2,6},{4,0},{6,2},{8,12},{10,14},{12,8},{14,10},{16,20},{18,... | collective-permute-start | bytes 700424 | tf_op jit(solution)/shard_map/ppermute | solution.py:88
  93.3 9.0 %collective-permute-start.20 = (f32[152,384]{1,0:T(8,128)S(1)}, f32[152,384]{1,0:T(8,128)S(1)}, u32[]{:S(2)}, u32[]{:S(2)}) collective-permute-start(f32[152,384]{1,0:T(8,128)S(1)} %get-tuple-element.33), channel_id=1, source_target_pairs={{0,2},{2,0},{4,6},{6,4},{8,10},{10,8},{12,14},{14,12},{16,18},{18,... | collective-permute-start | bytes 700424 | tf_op jit(solution)/shard_map/ppermute | solution.py:88
  93.4 10.6 %collective-permute-start.17 = (f32[152,384]{1,0:T(8,128)S(1)}, f32[152,384]{1,0:T(8,128)S(1)}, u32[]{:S(2)}, u32[]{:S(2)}) collective-permute-start(f32[152,384]{1,0:T(8,128)S(1)} %get-tuple-element.31), channel_id=1, source_target_pairs={{0,4},{2,6},{4,0},{6,2},{8,12},{10,14},{12,8},{14,10},{16,20},{18,... | collective-permute-start | bytes 700424 | tf_op jit(solution)/shard_map/ppermute | solution.py:88
  100.3 8.6 %collective-permute-start.19 = (f32[152,384]{1,0:T(8,128)S(1)}, f32[152,384]{1,0:T(8,128)S(1)}, u32[]{:S(2)}, u32[]{:S(2)}) collective-permute-start(f32[152,384]{1,0:T(8,128)S(1)} %get-tuple-element.32), channel_id=1, source_target_pairs={{0,2},{2,0},{4,6},{6,4},{8,10},{10,8},{12,14},{14,12},{16,18},{18,... | collective-permute-start | bytes 700424 | tf_op jit(solution)/shard_map/ppermute | solution.py:88
  106.4 9.1 %collective-permute-start.18 = (f32[152,384]{1,0:T(8,128)S(1)}, f32[152,384]{1,0:T(8,128)S(1)}, u32[]{:S(2)}, u32[]{:S(2)}) collective-permute-start(f32[152,384]{1,0:T(8,128)S(1)} %add_add_fusion.3), channel_id=1, source_target_pairs={{0,16},{2,18},{4,20},{6,22},{8,24},{10,26},{12,28},{14,30},{16,0},... | collective-permute-start | bytes 700424 | tf_op jit(solution)/shard_map/ppermute | solution.py:88
  123.9 8.5 %collective-permute-start.23 = (f32[152,384]{1,0:T(8,128)S(1)}, f32[152,384]{1,0:T(8,128)S(1)}, u32[]{:S(2)}, u32[]{:S(2)}) collective-permute-start(f32[152,384]{1,0:T(8,128)S(1)} %residual.2.refs_0_), channel_id=1, source_target_pairs={{0,16},{2,18},{4,20},{6,22},{8,24},{10,26},{12,28},{14,30},{16,0},... | collective-permute-start | bytes 700424 | tf_op jit(solution)/shard_map/ppermute | solution.py:88
  124.0 11.8 %collective-permute-start.26 = (f32[152,384]{1,0:T(8,128)S(1)}, f32[152,384]{1,0:T(8,128)S(1)}, u32[]{:S(2)}, u32[]{:S(2)}) collective-permute-start(f32[152,384]{1,0:T(8,128)S(1)} %residual.2.refs_0_), channel_id=1, source_target_pairs={{0,4},{2,6},{4,0},{6,2},{8,12},{10,14},{12,8},{14,10},{16,20},{18,... | collective-permute-start | bytes 700424 | tf_op jit(solution)/shard_map/ppermute | solution.py:88
  126.0 10.9 %collective-permute-start.29 = (f32[152,384]{1,0:T(8,128)S(1)}, f32[152,384]{1,0:T(8,128)S(1)}, u32[]{:S(2)}, u32[]{:S(2)}) collective-permute-start(f32[152,384]{1,0:T(8,128)S(1)} %residual.2.refs_0_), channel_id=1, source_target_pairs={{0,2},{2,0},{4,6},{6,4},{8,10},{10,8},{12,14},{14,12},{16,18},{18,... | collective-permute-start | bytes 700424 | tf_op jit(solution)/shard_map/ppermute | solution.py:88
  158.8 8.3 %collective-permute-start.34 = (f32[1,1]{1,0:T(1,128)}, f32[1,1]{1,0:T(1,128)}, u32[]{:S(2)}, u32[]{:S(2)}) collective-permute-start(f32[1,1]{1,0:T(1,128)} %add.125), channel_id=1, source_target_pairs={{0,8},{2,10},{4,12},{6,14},{8,0},{10,2},{12,4},{14,6},{16,24},{18,... | collective-permute-start | bytes 20 | tf_op jit(solution)/shard_map/ppermute | solution.py:110
  173.6 9.6 %collective-permute-start.37 = (f32[152,384]{1,0:T(8,128)S(1)}, f32[152,384]{1,0:T(8,128)S(1)}, u32[]{:S(2)}, u32[]{:S(2)}) collective-permute-start(f32[152,384]{1,0:T(8,128)S(1)} %scores.5._), channel_id=1, source_target_pairs={{0,4},{2,6},{4,0},{6,2},{8,12},{10,14},{12,8},{14,10},{16,20},{18,... | collective-permute-start | bytes 700424 | tf_op jit(solution)/shard_map/ppermute | solution.py:88
  180.5 8.5 %collective-permute-start.42 = (f32[152,384]{1,0:T(8,128)S(1)}, f32[152,384]{1,0:T(8,128)S(1)}, u32[]{:S(2)}, u32[]{:S(2)}) collective-permute-start(f32[152,384]{1,0:T(8,128)S(1)} %get-tuple-element.49), channel_id=1, source_target_pairs={{0,2},{2,0},{4,6},{6,4},{8,10},{10,8},{12,14},{14,12},{16,18},{18,... | collective-permute-start | bytes 700424 | tf_op jit(solution)/shard_map/ppermute | solution.py:88
  182.1 8.3 %collective-permute-start.39 = (f32[152,384]{1,0:T(8,128)S(1)}, f32[152,384]{1,0:T(8,128)S(1)}, u32[]{:S(2)}, u32[]{:S(2)}) collective-permute-start(f32[152,384]{1,0:T(8,128)S(1)} %get-tuple-element.47), channel_id=1, source_target_pairs={{0,4},{2,6},{4,0},{6,2},{8,12},{10,14},{12,8},{14,10},{16,20},{18,... | collective-permute-start | bytes 700424 | tf_op jit(solution)/shard_map/ppermute | solution.py:88
  191.6 8.7 %collective-permute-start.40 = (f32[152,384]{1,0:T(8,128)S(1)}, f32[152,384]{1,0:T(8,128)S(1)}, u32[]{:S(2)}, u32[]{:S(2)}) collective-permute-start(f32[152,384]{1,0:T(8,128)S(1)} %add_add_fusion.1), channel_id=1, source_target_pairs={{0,16},{2,18},{4,20},{6,22},{8,24},{10,26},{12,28},{14,30},{16,0},... | collective-permute-start | bytes 700424 | tf_op jit(solution)/shard_map/ppermute | solution.py:88
  208.5 8.5 %collective-permute-start.45 = (f32[152,384]{1,0:T(8,128)S(1)}, f32[152,384]{1,0:T(8,128)S(1)}, u32[]{:S(2)}, u32[]{:S(2)}) collective-permute-start(f32[152,384]{1,0:T(8,128)S(1)} %residual.3.refs_0_), channel_id=1, source_target_pairs={{0,16},{2,18},{4,20},{6,22},{8,24},{10,26},{12,28},{14,30},{16,0},... | collective-permute-start | bytes 700424 | tf_op jit(solution)/shard_map/ppermute | solution.py:88
  208.6 12.6 %collective-permute-start.48 = (f32[152,384]{1,0:T(8,128)S(1)}, f32[152,384]{1,0:T(8,128)S(1)}, u32[]{:S(2)}, u32[]{:S(2)}) collective-permute-start(f32[152,384]{1,0:T(8,128)S(1)} %residual.3.refs_0_), channel_id=1, source_target_pairs={{0,4},{2,6},{4,0},{6,2},{8,12},{10,14},{12,8},{14,10},{16,20},{18,... | collective-permute-start | bytes 700424 | tf_op jit(solution)/shard_map/ppermute | solution.py:88
  209.5 12.2 %collective-permute-start.51 = (f32[152,384]{1,0:T(8,128)S(1)}, f32[152,384]{1,0:T(8,128)S(1)}, u32[]{:S(2)}, u32[]{:S(2)}) collective-permute-start(f32[152,384]{1,0:T(8,128)S(1)} %residual.3.refs_0_), channel_id=1, source_target_pairs={{0,2},{2,0},{4,6},{6,4},{8,10},{10,8},{12,14},{14,12},{16,18},{18,... | collective-permute-start | bytes 700424 | tf_op jit(solution)/shard_map/ppermute | solution.py:88
  244.2 8.3 %collective-permute-start.56 = (f32[1,1]{1,0:T(1,128)}, f32[1,1]{1,0:T(1,128)}, u32[]{:S(2)}, u32[]{:S(2)}) collective-permute-start(f32[1,1]{1,0:T(1,128)} %add.142), channel_id=1, source_target_pairs={{0,8},{2,10},{4,12},{6,14},{8,0},{10,2},{12,4},{14,6},{16,24},{18,... | collective-permute-start | bytes 20 | tf_op jit(solution)/shard_map/ppermute | solution.py:110
  (34 other events, 245.9 us)
